TPU v7x, 32 devices: a whole 2x2x4 slice. The times are simulated.
32 devices in a mesh: dp: 4 (over y, x), mp: 8 (over z, core).
Axes of the slice: x: 2, y: 2, z: 4, core: 2. Of those that a mesh axis runs over, the one named last changes fastest.
Arguments:
- out_grads: bfloat16 [512, 28672], P('dp', 'mp'), may hold values from -6 to 6
- inputs: bfloat16 [512, 8192], P('mp', 'dp'), may hold values from -6 to 6
- out_basis: bfloat16 [28672, 14336], P('mp', 'dp'), may hold values from -0.03125 to 0.03125
- in_basis: bfloat16 [8192, 8192], P('dp', 'mp'), may hold values from -0.0625 to 0.0625
- query_out: bfloat16 [128, 28672], P('dp', 'mp'), may hold values from -2.390625 to 2.390625
- query_in: bfloat16 [128, 8192], P('mp', 'dp'), may hold values from -2.390625 to 2.390625
- damping: float32 [1], replicated, may hold values from 0.5 to 2
Outputs:
- eigenvalues: float32 [14336, 8192], P('dp', 'mp')
- preconditioned: bfloat16 [4, 14336, 8192], P(None, 'dp', 'mp')
All inputs are finite; a program needn't handle non-finite values.
Results may differ from a plain program's by a relative error of at most 0.033.
Values may be sent and summed in bfloat16 or wider, within the bound.
No kernel may reach another device: no remote copies, remote signals or barrier semaphores. Data moves between devices by JAX's collectives and lax.ppermute only.
A program may use at most 128 MiB of HBM per device.

v0:
```python
import jax
import jax.numpy as jnp
from jax import lax
from jax.experimental import pallas as pl
from jax.experimental.pallas import tpu as pltpu
from jax.sharding import PartitionSpec as P

QUARTERS = 4
HALVES = 2
PIECES = QUARTERS * HALVES
MIB = 1 << 20
LANES = 128


def tile_of(width, limit):
    return max(t for t in range(LANES, limit + 1, LANES) if width % t == 0)


def contract_rows(left, right):
    return lax.dot_general(
        left, right, (((0,), (0,)), ((), ())), preferred_element_type=jnp.float32
    )


def add_rounded(left, right):
    return (left.astype(jnp.float32) + right.astype(jnp.float32)).astype(left.dtype)


def swap_quarter(x, bits):
    size = lax.axis_size("dp")
    step = bits * (size // QUARTERS)
    return lax.ppermute(x, "dp", [(i, i ^ step) for i in range(size)])


def swap_core(x):
    size = lax.axis_size("mp")
    return lax.ppermute(x, "mp", [(i, i ^ 1) for i in range(size)])


def move_chip(x, pairs):
    return lax.ppermute(
        x, "mp", [(HALVES * a + c, HALVES * b + c) for a, b in pairs for c in range(HALVES)]
    )


def line_sum(x):
    chips = lax.axis_size("mp") // HALVES
    last, inner = chips - 1, chips // 2
    chip = lax.axis_index("mp") // HALVES
    depth = jnp.minimum(chip, last - chip)
    for s in range(inner - 1):
        x = add_rounded(x, move_chip(x, [(s, s + 1), (last - s, last - s - 1)]))
    x = add_rounded(x, move_chip(x, [(inner - 1, inner), (inner, inner - 1)]))
    for s in range(inner - 1, 0, -1):
        came = move_chip(x, [(s, s - 1), (last - s, last - s + 1)])
        x = jnp.where(depth == s - 1, came, x)
    return x


def multiply_kernel(place_ref, low_ref, high_ref, basis_ref, keep_ref, send_ref, rows_ref):
    half = low_ref.shape[0]

    @pl.when(pl.program_id(0) == 0)
    def _():
        core = place_ref[1]
        rows_ref[pl.ds(pl.multiple_of(core * half, 16), half), :] = low_ref[...]
        rows_ref[pl.ds(pl.multiple_of((1 - core) * half, 16), half), :] = high_ref[...]

    terms = jnp.dot(rows_ref[...], basis_ref[...], preferred_element_type=jnp.float32)
    terms = terms.astype(keep_ref.dtype)
    keep_ref[...] = terms[:half]
    send_ref[...] = terms[half:]


def multiply(place, low, high, basis):
    half, depth = low.shape
    width = basis.shape[1]
    tile = tile_of(width, 512)
    rows = pl.BlockSpec((half, depth), lambda i: (0, 0))
    out = pl.BlockSpec((half, tile), lambda i: (0, i))
    return pl.pallas_call(
        multiply_kernel,
        grid=(width // tile,),
        in_specs=[
            pl.BlockSpec(memory_space=pltpu.SMEM),
            rows,
            rows,
            pl.BlockSpec((depth, tile), lambda i: (0, i)),
        ],
        out_specs=[out, out],
        out_shape=[jax.ShapeDtypeStruct((half, width), low.dtype)] * 2,
        scratch_shapes=[pltpu.VMEM((HALVES * half, depth), low.dtype)],
        compiler_params=pltpu.CompilerParams(vmem_limit_bytes=32 * MIB),
        cost_estimate=pl.CostEstimate(
            flops=4 * half * depth * width,
            bytes_accessed=2 * depth * width,
            transcendentals=0,
        ),
        name="multiply",
    )(place, low, high, basis)


def rotated_places(core):
    return [(0, core), (2 - core, core), (1 + core, core), (3, core)]


def correct_kernel(tokens, place_ref, damping_ref, *refs):
    groups = 2 * QUARTERS
    rot_refs, act_refs = refs[:groups], refs[groups:groups + HALVES]
    eig_ref, pre_ref, rot_tok, rot_qry, act_tok, act_qry = refs[groups + HALVES:]
    queries = rot_refs[0].shape[0] - tokens
    quarter, core = place_ref[0], place_ref[1]

    def put(tok, qry, piece, values):
        tok[pl.ds(pl.multiple_of(piece * tokens, 16), tokens), :] = values[:tokens]
        qry[pl.ds(pl.multiple_of(piece * queries, 16), queries), :] = values[tokens:]

    @pl.when(pl.program_id(0) == 0)
    def _():
        per_ref = PIECES // HALVES
        size = tokens + queries
        for piece in range(PIECES):
            at = piece % per_ref * size
            put(act_tok, act_qry, piece, act_refs[piece // per_ref][at:at + size, :])

    for held, refs_held in ((core, rot_refs[:QUARTERS]), (1 - core, rot_refs[QUARTERS:])):
        for (bits, half), ref in zip(rotated_places(held), refs_held):
            put(rot_tok, rot_qry, (quarter ^ bits) * HALVES + half, ref[...])

    length = tokens * PIECES // 2
    total = None
    for seq in range(2):
        rows = slice(seq * length, (seq + 1) * length)
        rotated = contract_rows(rot_tok[rows, :], act_tok[rows, :])
        square = rotated * rotated
        total = square if total is None else total + square
    eig = total * (1.0 / (2 * length))
    eig_ref[...] = eig
    inverse = 1.0 / (eig + damping_ref[0])
    rank = queries * HALVES
    for query in range(QUARTERS):
        rows = slice(query * rank, (query + 1) * rank)
        product = contract_rows(rot_qry[rows, :], act_qry[rows, :])
        pre_ref[query] = (product * inverse).astype(pre_ref.dtype)


def correct(tokens, place, damping, rot, act):
    size, outs = rot[0].shape
    rows, ins = act[0].shape
    queries = size - tokens
    tile = tile_of(outs, 256)
    smem = pl.BlockSpec(memory_space=pltpu.SMEM)
    dtype = rot[0].dtype
    return pl.pallas_call(
        lambda *refs: correct_kernel(tokens, *refs),
        grid=(outs // tile,),
        in_specs=[smem, smem]
        + [pl.BlockSpec((size, tile), lambda i: (0, i))] * len(rot)
        + [pl.BlockSpec((rows, ins), lambda i: (0, 0))] * len(act),
        out_specs=[
            pl.BlockSpec((tile, ins), lambda i: (i, 0)),
            pl.BlockSpec((QUARTERS, tile, ins), lambda i: (0, i, 0)),
        ],
        out_shape=[
            jax.ShapeDtypeStruct((outs, ins), jnp.float32),
            jax.ShapeDtypeStruct((QUARTERS, outs, ins), dtype),
        ],
        scratch_shapes=[
            pltpu.VMEM((PIECES * tokens, tile), dtype),
            pltpu.VMEM((PIECES * queries, tile), dtype),
            pltpu.VMEM((PIECES * tokens, ins), dtype),
            pltpu.VMEM((PIECES * queries, ins), dtype),
        ],
        compiler_params=pltpu.CompilerParams(vmem_limit_bytes=40 * MIB),
        cost_estimate=pl.CostEstimate(
            flops=2 * PIECES * size * outs * ins,
            bytes_accessed=12 * outs * ins,
            transcendentals=0,
        ),
        name="correct",
    )(place, damping, *rot, *act)


def outer_rows(tokens, queries):
    size = lax.axis_size("dp")
    index = lax.axis_index("dp")
    step = 1
    while step < size // QUARTERS:
        pairs = [(i, i ^ step) for i in range(size)]
        first = (index // step) % 2 == 0

        def joined(x):
            other = lax.ppermute(x, "dp", pairs)
            return jnp.where(
                first, jnp.concatenate([x, other]), jnp.concatenate([other, x])
            )

        tokens, queries = joined(tokens), joined(queries)
        step *= 2
    return tokens, queries


def quarter_sum(low, high):
    size = lax.axis_size("dp")
    for bits in (1, 2):
        low = add_rounded(low, swap_quarter(low, bits))
        high = add_rounded(high, swap_quarter(high, 3 - bits))
    step = 1
    while step < size // QUARTERS:
        pairs = [(i, i ^ step) for i in range(size)]
        low = add_rounded(low, lax.ppermute(low, "dp", pairs))
        high = add_rounded(high, lax.ppermute(high, "dp", pairs))
        step *= 2
    return low, high


def activation_rows(inputs, query_in):
    tokens = inputs.shape[0]
    blocks = lax.all_gather(jnp.concatenate([inputs, query_in]), "mp", axis=0)
    holders, _, width = blocks.shape
    if holders != PIECES:
        blocks = jnp.concatenate(
            [
                blocks[:, :tokens].reshape(PIECES, -1, width),
                blocks[:, tokens:].reshape(PIECES, -1, width),
            ],
            axis=1,
        )
    return blocks.reshape(-1, width)


def shards(out_grads, inputs, out_basis, in_basis, query_out, query_in, damping):
    dp = lax.axis_size("dp")
    place = jnp.stack(
        [lax.axis_index("dp") // (dp // QUARTERS), lax.axis_index("mp") % HALVES]
    ).astype(jnp.int32)

    act_rows = activation_rows(inputs, query_in)

    tokens, queries = outer_rows(out_grads, query_out)
    length = tokens.shape[0] // HALVES
    rank = queries.shape[0] // HALVES
    own = [
        jnp.concatenate(
            [tokens[h * length:(h + 1) * length], queries[h * rank:(h + 1) * rank]]
        )
        for h in range(HALVES)
    ]
    beside = [swap_quarter(own[0], 2), swap_quarter(own[1], 1)]
    behind = [swap_quarter(own[0], 1), swap_quarter(own[1], 2)]
    across = [swap_quarter(beside[0], 1), swap_quarter(beside[1], 2)]

    held, handed = [], []
    for low, high in (own, beside, behind, across):
        keep, send = multiply(place, low, high, out_basis)
        total = line_sum(add_rounded(keep, swap_core(send)))
        held.append(total)
        handed.append(swap_core(total))

    act_terms = jnp.dot(act_rows, in_basis, preferred_element_type=jnp.float32)
    act_terms = act_terms.astype(jnp.bfloat16)
    cut = act_terms.shape[0] // HALVES
    act = quarter_sum(act_terms[:cut], act_terms[cut:])
    return tuple(correct(length, place, damping, held + handed, act))


def solution(mesh):
    placed = (
        P("dp", "mp"),
        P("mp", "dp"),
        P("mp", "dp"),
        P("dp", "mp"),
        P("dp", "mp"),
        P("mp", "dp"),
        P(),
    )
    return jax.shard_map(
        shards,
        mesh=mesh,
        in_specs=placed,
        out_specs=(P("dp", "mp"), P(None, "dp", "mp")),
        check_vma=False,
    )
```

profile of v0, /device:TPU:13, one launch (start us, length us, event | category | flops | bytes accessed | tf_op | source)
XLA Modules:
  0.0 216.7 jit_solution(6264548566359759489)
XLA Ops:
  7.2 1.0 fusion.2
  8.2 1.2 fusion.1
  9.5 1.3 collective-permute-start.10
  10.8 0.2 collective-permute-start.4
  11.0 1.3 collective-permute-start.11
  12.3 0.3 collective-permute-start.5
  12.6 0.7 pad_maximum_fusion.2
  13.5 12.6 %multiply.4 = (bf16[80,3584]{1,0:T(8,128)(2,1)S(1)}, bf16[80,3584]{1,0:T(8,128)(2,1)}) custom-call(s32[2]{0:T(128)S(1)} %pad_add_fusion.place_ref.refs_0_, bf16[80,3584]{1,0:T(8,128)(2,1)S(1)} %pad_maximum_fusion.low_ref, bf16[80,3584]{1,0:T(8,128)(2,1)S(1)} %pad_maximum_fusion.1.high_ref, bf16[3584,3584]{1,0:T(8,128)(2,1)} %basis_ref.7), custom_call_target="tpu_custom_call" | custom-call | flops 4110417920 | bytes 25690112 | tf_op jit(solution)/shard_map/multiply/pallas_call | solution.py:81
  26.1 1.9 collective-permute-start
  28.0 8.7 %collective-permute-done.11.high_ref = bf16[80,3584]{1,0:T(8,128)(2,1)} collective-permute-done((bf16[80,3584]{1,0:T(8,128)(2,1)S(1)}, bf16[80,3584]{1,0:T(8,128)(2,1)}, u32[]{:S(2)}, u32[]{:S(2)}) %collective-permute-start.11) | collective-permute-done | bytes 573472 | tf_op jit(solution)/shard_map/ppermute | solution.py:32
  36.7 12.0 %multiply.6 = (bf16[80,3584]{1,0:T(8,128)(2,1)S(1)}, bf16[80,3584]{1,0:T(8,128)(2,1)S(1)}) custom-call(s32[2]{0:T(128)S(1)} %pad_add_fusion.place_ref.refs_0_, bf16[80,3584]{1,0:T(8,128)(2,1)S(1)} %collective-permute-done.10.low_ref, bf16[80,3584]{1,0:T(8,128)(2,1)} %collective-permute-done.11.high_ref, bf16[3584,3584]{1,0:T(8,128)(2,1)} %basis_ref.7), custom_call_target="tpu_custom_call" | custom-call | flops 4110417920 | bytes 25690112 | tf_op jit(solution)/shard_map/multiply/pallas_call | solution.py:81
  48.7 1.9 collective-permute-start.12
  50.6 11.7 %multiply.5 = (bf16[80,3584]{1,0:T(8,128)(2,1)S(1)}, bf16[80,3584]{1,0:T(8,128)(2,1)S(1)}) custom-call(s32[2]{0:T(128)S(1)} %pad_add_fusion.place_ref.refs_0_, bf16[80,3584]{1,0:T(8,128)(2,1)S(1)} %collective-permute-done.4.low_ref, bf16[80,3584]{1,0:T(8,128)(2,1)S(1)} %collective-permute-done.5.high_ref, bf16[3584,3584]{1,0:T(8,128)(2,1)} %basis_ref.7), custom_call_target="tpu_custom_call" | custom-call | flops 4110417920 | bytes 25690112 | tf_op jit(solution)/shard_map/multiply/pallas_call | solution.py:81
  62.4 0.1 collective-permute-start.6
  62.5 1.2 add_convert_fusion.15
  63.7 1.3 collective-permute-start.1
  65.0 0.3 collective-permute-start.16
  65.3 0.2 collective-permute-start.17
  65.5 0.1 add_convert_fusion.9
  65.7 1.3 collective-permute-start.13
  67.0 0.1 add_convert_fusion.12
  67.1 1.3 collective-permute-start.7
  68.4 11.2 %collective-permute-done.1 = bf16[80,3584]{1,0:T(8,128)(2,1)S(1)} collective-permute-done((bf16[80,3584]{1,0:T(8,128)(2,1)S(1)}, bf16[80,3584]{1,0:T(8,128)(2,1)S(1)}, u32[]{:S(2)}, u32[]{:S(2)}) %collective-permute-start.1) | collective-permute-done | bytes 573472 | tf_op jit(solution)/shard_map/ppermute | solution.py:41
  79.6 0.1 add_convert_fusion.14
  79.8 3.2 %collective-permute-start.2 = (bf16[80,3584]{1,0:T(8,128)(2,1)S(1)}, bf16[80,3584]{1,0:T(8,128)(2,1)S(1)}, u32[]{:S(2)}, u32[]{:S(2)}) collective-permute-start(bf16[80,3584]{1,0:T(8,128)(2,1)S(1)} %add_convert_fusion.14), channel_id=1, source_target_pairs={{2,4},{3,5},{4,2},{5,3},{10,12},{11,13},{12,10},{13,11},{18,20},{1... | collective-permute-start | bytes 1720328 | tf_op jit(solution)/shard_map/ppermute | solution.py:41
  83.0 11.7 %multiply.7 = (bf16[80,3584]{1,0:T(8,128)(2,1)S(1)}, bf16[80,3584]{1,0:T(8,128)(2,1)S(1)}) custom-call(s32[2]{0:T(128)S(1)} %pad_add_fusion.place_ref.refs_0_, bf16[80,3584]{1,0:T(8,128)(2,1)S(1)} %collective-permute-done.16.low_ref, bf16[80,3584]{1,0:T(8,128)(2,1)S(1)} %collective-permute-done.17.high_ref, bf16[3584,3584]{1,0:T(8,128)(2,1)} %basis_ref.7), custom_call_target="tpu_custom_call" | custom-call | flops 4110417920 | bytes 25690112 | tf_op jit(solution)/shard_map/multiply/pallas_call | solution.py:81
  94.7 2.6 %collective-permute-start.18 = (bf16[80,3584]{1,0:T(8,128)(2,1)S(1)}, bf16[80,3584]{1,0:T(8,128)(2,1)S(1)}, u32[]{:S(2)}, u32[]{:S(2)}) collective-permute-start(bf16[80,3584]{1,0:T(8,128)(2,1)S(1)} %get-tuple-element.17), channel_id=1, source_target_pairs={{0,1},{1,0},{2,3},{3,2},{4,5},{5,4},{6,7},{7,6},{8,9},{9,8},{10,11... | collective-permute-start | bytes 1720328 | tf_op jit(solution)/shard_map/ppermute | solution.py:37
  97.3 0.1 add_convert_fusion.8
  97.4 2.1 collective-permute-start.14
  99.5 4.7 %collective-permute-done.7 = bf16[80,3584]{1,0:T(8,128)(2,1)S(1)} collective-permute-done((bf16[80,3584]{1,0:T(8,128)(2,1)S(1)}, bf16[80,3584]{1,0:T(8,128)(2,1)S(1)}, u32[]{:S(2)}, u32[]{:S(2)}) %collective-permute-start.7) | collective-permute-done | bytes 573472 | tf_op jit(solution)/shard_map/ppermute | solution.py:41
  104.2 0.1 add_convert_fusion.11
  104.3 3.2 %collective-permute-start.8 = (bf16[80,3584]{1,0:T(8,128)(2,1)S(1)}, bf16[80,3584]{1,0:T(8,128)(2,1)S(1)}, u32[]{:S(2)}, u32[]{:S(2)}) collective-permute-start(bf16[80,3584]{1,0:T(8,128)(2,1)S(1)} %add_convert_fusion.11), channel_id=1, source_target_pairs={{2,4},{3,5},{4,2},{5,3},{10,12},{11,13},{12,10},{13,11},{18,20},{1... | collective-permute-start | bytes 1720328 | tf_op jit(solution)/shard_map/ppermute | solution.py:41
  107.5 0.1 add_convert_fusion.13
  107.7 1.3 collective-permute-start.3
  109.0 0.1 add_convert_fusion.6
  109.2 1.3 collective-permute-start.19
  110.5 3.4 %collective-permute-done.14 = bf16[80,3584]{1,0:T(8,128)(2,1)S(1)} collective-permute-done((bf16[80,3584]{1,0:T(8,128)(2,1)S(1)}, bf16[80,3584]{1,0:T(8,128)(2,1)S(1)}, u32[]{:S(2)}, u32[]{:S(2)}) %collective-permute-start.14) | collective-permute-done | bytes 573472 | tf_op jit(solution)/shard_map/ppermute | solution.py:41
  113.9 0.1 add_convert_fusion.7
  114.1 1.3 collective-permute-start.15
  115.4 10.8 %collective-permute-done.8 = bf16[80,3584]{1,0:T(8,128)(2,1)S(1)} collective-permute-done((bf16[80,3584]{1,0:T(8,128)(2,1)S(1)}, bf16[80,3584]{1,0:T(8,128)(2,1)S(1)}, u32[]{:S(2)}, u32[]{:S(2)}) %collective-permute-start.8) | collective-permute-done | bytes 573472 | tf_op jit(solution)/shard_map/ppermute | solution.py:41
  126.2 0.1 add_convert_fusion.10
  126.3 2.1 collective-permute-start.9
  128.6 0.9 collective-permute-start.22
  129.4 0.1 add_convert_fusion.5
  129.6 2.1 collective-permute-start.20
  131.7 0.5 collective-permute-done.15
  132.3 4.2 %collective-permute-start.24 = (bf16[80,3584]{1,0:T(8,128)(2,1)S(1)}, bf16[80,3584]{1,0:T(8,128)(2,1)S(1)}, u32[]{:S(2)}, u32[]{:S(2)}) collective-permute-start(bf16[80,3584]{1,0:T(8,128)(2,1)S(1)} %broadcast_select_fusion.1.refs_4_), channel_id=1, source_target_pairs={{0,1},{1,0},{2,3},{3,2},{4,5},{5,4},{6,7},{7,6},{8,9},{9,8},{10,11... | collective-permute-start | bytes 1720328 | tf_op jit(solution)/shard_map/ppermute | solution.py:37
  136.4 9.6 %collective-permute-done.20 = bf16[80,3584]{1,0:T(8,128)(2,1)S(1)} collective-permute-done((bf16[80,3584]{1,0:T(8,128)(2,1)S(1)}, bf16[80,3584]{1,0:T(8,128)(2,1)S(1)}, u32[]{:S(2)}, u32[]{:S(2)}) %collective-permute-start.20) | collective-permute-done | bytes 573472 | tf_op jit(solution)/shard_map/ppermute | solution.py:41
  146.1 0.1 add_convert_fusion.4
  146.2 2.1 collective-permute-start.21
  148.3 5.9 %convolution_convert_fusion = bf16[640,1024]{1,0:T(8,128)(2,1)S(1)} fusion(bf16[640,2048]{1,0:T(8,128)(2,1)} %all-gather.3.cloned.1.call-done, bf16[2048,1024]{1,0:T(8,128)(2,1)} %param.10), kind=kOutput, calls=%fused_computation | convolution fusion | flops 2685009920 | bytes 8126464 | tf_op jit(solution)/shard_map/dot_general | solution.py:260
  154.3 0.3 collective-permute-start.28
  154.6 0.3 collective-permute-start.26
  154.9 14.9 %collective-permute-done.28 = bf16[320,1024]{1,0:T(8,128)(2,1)S(1)} collective-permute-done((bf16[320,1024]{1,0:T(8,128)(2,1)S(1)}, bf16[320,1024]{1,0:T(8,128)(2,1)S(1)}, u32[]{:S(2)}, u32[]{:S(2)}) %collective-permute-start.28) | collective-permute-done | bytes 655392 | tf_op jit(solution)/shard_map/ppermute | solution.py:32
  169.8 1.7 collective-permute-start.23
  171.5 0.5 add_convert_fusion.1
  172.0 0.3 collective-permute-start.29
  172.4 0.2 collective-permute-start.27
  172.7 15.5 %collective-permute-done.29 = bf16[320,1024]{1,0:T(8,128)(2,1)S(1)} collective-permute-done((bf16[320,1024]{1,0:T(8,128)(2,1)S(1)}, bf16[320,1024]{1,0:T(8,128)(2,1)S(1)}, u32[]{:S(2)}, u32[]{:S(2)}) %collective-permute-start.29) | collective-permute-done | bytes 655392 | tf_op jit(solution)/shard_map/ppermute | solution.py:32
  188.2 1.0 collective-permute-start.25
  189.9 0.2 add_convert_fusion.refs_11_
  190.1 0.2 add_convert_fusion.2.refs_10_
  190.4 0.4 collective-permute-done.25.refs_9_
  190.8 19.0 %correct.1 = (f32[3584,1024]{1,0:T(8,128)}, bf16[4,3584,1024]{2,1,0:T(8,128)(2,1)}) custom-call(s32[2]{0:T(128)S(1)} %pad_add_fusion.place_ref.refs_0_, f32[1]{0:T(128)S(6)} %copy.9.refs_1_, bf16[80,3584]{1,0:T(8,128)(2,1)S(1)} %broadcast_select_fusion.3.refs_2_, bf16[80,3584]{1,0:T(8,128)(2,1)S(1)} %broadcast_select_fusion.2.refs_3_, ...), custom_call_target="tpu_custom_call" | custom-call | flops 4697620480 | bytes 44040192 | tf_op jit(solution)/shard_map/correct/pallas_call | solution.py:154
  (35 shorter events, 0.7 us)
Async XLA Ops:
  7.2 141.2 %all-gather.3.cloned.1.call-start = ((), (), s32[]{:S(2)}) async-start(), calls=%async_computation | async-start | bytes 2949120 | tf_op jit(solution)/shard_map/all_gather | solution.py:219
  9.4 3.2 %copy-start = (bf16[64,2048]{1,0:T(8,128)(2,1)S(1)}, bf16[64,2048]{1,0:T(8,128)(2,1)}, u32[]{:S(2)}) copy-start(bf16[64,2048]{1,0:T(8,128)(2,1)} %param.8) | copy-start | bytes 786436
  9.4 3.2 %copy-start.1 = (bf16[16,2048]{1,0:T(8,128)(2,1)S(1)}, bf16[16,2048]{1,0:T(8,128)(2,1)}, u32[]{:S(2)}) copy-start(bf16[16,2048]{1,0:T(8,128)(2,1)} %param.12) | copy-start | bytes 196612
  9.5 18.5 %collective-permute-start.10 = (bf16[80,3584]{1,0:T(8,128)(2,1)S(1)}, bf16[80,3584]{1,0:T(8,128)(2,1)S(1)}, u32[]{:S(2)}, u32[]{:S(2)}) collective-permute-start(bf16[80,3584]{1,0:T(8,128)(2,1)S(1)} %pad_maximum_fusion.low_ref), channel_id=1, source_target_pairs={{0,8},{8,0},{16,24},{24,16},{1,9},{9,1},{17,25},{25,17},{2,10},{10... | collective-permute-start | bytes 1720328 | tf_op jit(solution)/shard_map/ppermute | solution.py:32
  10.8 39.9 %collective-permute-start.4 = (bf16[80,3584]{1,0:T(8,128)(2,1)S(1)}, bf16[80,3584]{1,0:T(8,128)(2,1)S(1)}, u32[]{:S(2)}, u32[]{:S(2)}) collective-permute-start(bf16[80,3584]{1,0:T(8,128)(2,1)S(1)} %pad_maximum_fusion.low_ref), channel_id=1, source_target_pairs={{0,16},{8,24},{16,0},{24,8},{1,17},{9,25},{17,1},{25,9},{2,18},{10... | collective-permute-start | bytes 1720328 | tf_op jit(solution)/shard_map/ppermute | solution.py:32
  11.0 25.7 %collective-permute-start.11 = (bf16[80,3584]{1,0:T(8,128)(2,1)S(1)}, bf16[80,3584]{1,0:T(8,128)(2,1)}, u32[]{:S(2)}, u32[]{:S(2)}) collective-permute-start(bf16[80,3584]{1,0:T(8,128)(2,1)S(1)} %pad_maximum_fusion.1.high_ref), channel_id=1, source_target_pairs={{0,16},{8,24},{16,0},{24,8},{1,17},{9,25},{17,1},{25,9},{2,18},{10... | collective-permute-start | bytes 1720328 | tf_op jit(solution)/shard_map/ppermute | solution.py:32
  12.3 38.3 %collective-permute-start.5 = (bf16[80,3584]{1,0:T(8,128)(2,1)S(1)}, bf16[80,3584]{1,0:T(8,128)(2,1)S(1)}, u32[]{:S(2)}, u32[]{:S(2)}) collective-permute-start(bf16[80,3584]{1,0:T(8,128)(2,1)S(1)} %pad_maximum_fusion.1.high_ref), channel_id=1, source_target_pairs={{0,8},{8,0},{16,24},{24,16},{1,9},{9,1},{17,25},{25,17},{2,10},{10... | collective-permute-start | bytes 1720328 | tf_op jit(solution)/shard_map/ppermute | solution.py:32
  26.1 36.4 %collective-permute-start = (bf16[80,3584]{1,0:T(8,128)(2,1)}, bf16[80,3584]{1,0:T(8,128)(2,1)}, u32[]{:S(2)}, u32[]{:S(2)}) collective-permute-start(bf16[80,3584]{1,0:T(8,128)(2,1)} %get-tuple-element.11), channel_id=1, source_target_pairs={{0,1},{1,0},{2,3},{3,2},{4,5},{5,4},{6,7},{7,6},{8,9},{9,8},{10,11... | collective-permute-start | bytes 1720328 | tf_op jit(solution)/shard_map/ppermute | solution.py:37
  48.7 16.8 %collective-permute-start.12 = (bf16[80,3584]{1,0:T(8,128)(2,1)S(1)}, bf16[80,3584]{1,0:T(8,128)(2,1)S(1)}, u32[]{:S(2)}, u32[]{:S(2)}) collective-permute-start(bf16[80,3584]{1,0:T(8,128)(2,1)S(1)} %get-tuple-element.15), channel_id=1, source_target_pairs={{0,1},{1,0},{2,3},{3,2},{4,5},{5,4},{6,7},{7,6},{8,9},{9,8},{10,11... | collective-permute-start | bytes 1720328 | tf_op jit(solution)/shard_map/ppermute | solution.py:37
  62.4 4.6 %collective-permute-start.6 = (bf16[80,3584]{1,0:T(8,128)(2,1)S(1)}, bf16[80,3584]{1,0:T(8,128)(2,1)S(1)}, u32[]{:S(2)}, u32[]{:S(2)}) collective-permute-start(bf16[80,3584]{1,0:T(8,128)(2,1)S(1)} %get-tuple-element.13), channel_id=1, source_target_pairs={{0,1},{1,0},{2,3},{3,2},{4,5},{5,4},{6,7},{7,6},{8,9},{9,8},{10,11... | collective-permute-start | bytes 1720328 | tf_op jit(solution)/shard_map/ppermute | solution.py:37
  63.7 16.0 %collective-permute-start.1 = (bf16[80,3584]{1,0:T(8,128)(2,1)S(1)}, bf16[80,3584]{1,0:T(8,128)(2,1)S(1)}, u32[]{:S(2)}, u32[]{:S(2)}) collective-permute-start(bf16[80,3584]{1,0:T(8,128)(2,1)S(1)} %add_convert_fusion.15), channel_id=1, source_target_pairs={{0,2},{1,3},{6,4},{7,5},{8,10},{9,11},{14,12},{15,13},{16,18},{17,... | collective-permute-start | bytes 1720328 | tf_op jit(solution)/shard_map/ppermute | solution.py:41
  65.0 18.0 %collective-permute-start.16 = (bf16[80,3584]{1,0:T(8,128)(2,1)S(1)}, bf16[80,3584]{1,0:T(8,128)(2,1)S(1)}, u32[]{:S(2)}, u32[]{:S(2)}) collective-permute-start(bf16[80,3584]{1,0:T(8,128)(2,1)S(1)} %collective-permute-done.4.low_ref), channel_id=1, source_target_pairs={{0,8},{8,0},{16,24},{24,16},{1,9},{9,1},{17,25},{25,17},{2,10},{10... | collective-permute-start | bytes 1720328 | tf_op jit(solution)/shard_map/ppermute | solution.py:32
  65.3 17.7 %collective-permute-start.17 = (bf16[80,3584]{1,0:T(8,128)(2,1)S(1)}, bf16[80,3584]{1,0:T(8,128)(2,1)S(1)}, u32[]{:S(2)}, u32[]{:S(2)}) collective-permute-start(bf16[80,3584]{1,0:T(8,128)(2,1)S(1)} %collective-permute-done.5.high_ref), channel_id=1, source_target_pairs={{0,16},{8,24},{16,0},{24,8},{1,17},{9,25},{17,1},{25,9},{2,18},{10... | collective-permute-start | bytes 1720328 | tf_op jit(solution)/shard_map/ppermute | solution.py:32
  65.7 31.6 %collective-permute-start.13 = (bf16[80,3584]{1,0:T(8,128)(2,1)S(1)}, bf16[80,3584]{1,0:T(8,128)(2,1)S(1)}, u32[]{:S(2)}, u32[]{:S(2)}) collective-permute-start(bf16[80,3584]{1,0:T(8,128)(2,1)S(1)} %add_convert_fusion.9), channel_id=1, source_target_pairs={{0,2},{1,3},{6,4},{7,5},{8,10},{9,11},{14,12},{15,13},{16,18},{17,... | collective-permute-start | bytes 1720328 | tf_op jit(solution)/shard_map/ppermute | solution.py:41
  67.1 37.1 %collective-permute-start.7 = (bf16[80,3584]{1,0:T(8,128)(2,1)S(1)}, bf16[80,3584]{1,0:T(8,128)(2,1)S(1)}, u32[]{:S(2)}, u32[]{:S(2)}) collective-permute-start(bf16[80,3584]{1,0:T(8,128)(2,1)S(1)} %add_convert_fusion.12), channel_id=1, source_target_pairs={{0,2},{1,3},{6,4},{7,5},{8,10},{9,11},{14,12},{15,13},{16,18},{17,... | collective-permute-start | bytes 1720328 | tf_op jit(solution)/shard_map/ppermute | solution.py:41
  79.8 27.8 %collective-permute-start.2 = (bf16[80,3584]{1,0:T(8,128)(2,1)S(1)}, bf16[80,3584]{1,0:T(8,128)(2,1)S(1)}, u32[]{:S(2)}, u32[]{:S(2)}) collective-permute-start(bf16[80,3584]{1,0:T(8,128)(2,1)S(1)} %add_convert_fusion.14), channel_id=1, source_target_pairs={{2,4},{3,5},{4,2},{5,3},{10,12},{11,13},{12,10},{13,11},{18,20},{1... | collective-permute-start | bytes 1720328 | tf_op jit(solution)/shard_map/ppermute | solution.py:41
  94.7 14.3 %collective-permute-start.18 = (bf16[80,3584]{1,0:T(8,128)(2,1)S(1)}, bf16[80,3584]{1,0:T(8,128)(2,1)S(1)}, u32[]{:S(2)}, u32[]{:S(2)}) collective-permute-start(bf16[80,3584]{1,0:T(8,128)(2,1)S(1)} %get-tuple-element.17), channel_id=1, source_target_pairs={{0,1},{1,0},{2,3},{3,2},{4,5},{5,4},{6,7},{7,6},{8,9},{9,8},{10,11... | collective-permute-start | bytes 1720328 | tf_op jit(solution)/shard_map/ppermute | solution.py:37
  97.4 16.5 %collective-permute-start.14 = (bf16[80,3584]{1,0:T(8,128)(2,1)S(1)}, bf16[80,3584]{1,0:T(8,128)(2,1)S(1)}, u32[]{:S(2)}, u32[]{:S(2)}) collective-permute-start(bf16[80,3584]{1,0:T(8,128)(2,1)S(1)} %add_convert_fusion.8), channel_id=1, source_target_pairs={{2,4},{3,5},{4,2},{5,3},{10,12},{11,13},{12,10},{13,11},{18,20},{1... | collective-permute-start | bytes 1720328 | tf_op jit(solution)/shard_map/ppermute | solution.py:41
  104.3 21.9 %collective-permute-start.8 = (bf16[80,3584]{1,0:T(8,128)(2,1)S(1)}, bf16[80,3584]{1,0:T(8,128)(2,1)S(1)}, u32[]{:S(2)}, u32[]{:S(2)}) collective-permute-start(bf16[80,3584]{1,0:T(8,128)(2,1)S(1)} %add_convert_fusion.11), channel_id=1, source_target_pairs={{2,4},{3,5},{4,2},{5,3},{10,12},{11,13},{12,10},{13,11},{18,20},{1... | collective-permute-start | bytes 1720328 | tf_op jit(solution)/shard_map/ppermute | solution.py:41
  107.7 20.8 %collective-permute-start.3 = (bf16[80,3584]{1,0:T(8,128)(2,1)S(1)}, bf16[80,3584]{1,0:T(8,128)(2,1)S(1)}, u32[]{:S(2)}, u32[]{:S(2)}) collective-permute-start(bf16[80,3584]{1,0:T(8,128)(2,1)S(1)} %add_convert_fusion.13), channel_id=1, source_target_pairs={{2,0},{3,1},{4,6},{5,7},{10,8},{11,9},{12,14},{13,15},{18,16},{19,... | collective-permute-start | bytes 1720328 | tf_op jit(solution)/shard_map/ppermute | solution.py:41
  109.2 20.3 %collective-permute-start.19 = (bf16[80,3584]{1,0:T(8,128)(2,1)S(1)}, bf16[80,3584]{1,0:T(8,128)(2,1)S(1)}, u32[]{:S(2)}, u32[]{:S(2)}) collective-permute-start(bf16[80,3584]{1,0:T(8,128)(2,1)S(1)} %add_convert_fusion.6), channel_id=1, source_target_pairs={{0,2},{1,3},{6,4},{7,5},{8,10},{9,11},{14,12},{15,13},{16,18},{17,... | collective-permute-start | bytes 1720328 | tf_op jit(solution)/shard_map/ppermute | solution.py:41
  114.1 18.1 %collective-permute-start.15 = (bf16[80,3584]{1,0:T(8,128)(2,1)S(1)}, bf16[80,3584]{1,0:T(8,128)(2,1)S(1)}, u32[]{:S(2)}, u32[]{:S(2)}) collective-permute-start(bf16[80,3584]{1,0:T(8,128)(2,1)S(1)} %add_convert_fusion.7), channel_id=1, source_target_pairs={{2,0},{3,1},{4,6},{5,7},{10,8},{11,9},{12,14},{13,15},{18,16},{19,... | collective-permute-start | bytes 1720328 | tf_op jit(solution)/shard_map/ppermute | solution.py:41
  126.3 28.2 %collective-permute-start.9 = (bf16[80,3584]{1,0:T(8,128)(2,1)S(1)}, bf16[80,3584]{1,0:T(8,128)(2,1)}, u32[]{:S(2)}, u32[]{:S(2)}) collective-permute-start(bf16[80,3584]{1,0:T(8,128)(2,1)S(1)} %add_convert_fusion.10), channel_id=1, source_target_pairs={{2,0},{3,1},{4,6},{5,7},{10,8},{11,9},{12,14},{13,15},{18,16},{19,... | collective-permute-start | bytes 1720328 | tf_op jit(solution)/shard_map/ppermute | solution.py:41
  128.6 61.8 %collective-permute-start.22 = (bf16[80,3584]{1,0:T(8,128)(2,1)S(1)}, bf16[80,3584]{1,0:T(8,128)(2,1)S(1)}, u32[]{:S(2)}, u32[]{:S(2)}) collective-permute-start(bf16[80,3584]{1,0:T(8,128)(2,1)S(1)} %broadcast_select_fusion.3.refs_2_), channel_id=1, source_target_pairs={{0,1},{1,0},{2,3},{3,2},{4,5},{5,4},{6,7},{7,6},{8,9},{9,8},{10,11... | collective-permute-start | bytes 1720328 | tf_op jit(solution)/shard_map/ppermute | solution.py:37
  129.6 16.5 %collective-permute-start.20 = (bf16[80,3584]{1,0:T(8,128)(2,1)S(1)}, bf16[80,3584]{1,0:T(8,128)(2,1)S(1)}, u32[]{:S(2)}, u32[]{:S(2)}) collective-permute-start(bf16[80,3584]{1,0:T(8,128)(2,1)S(1)} %add_convert_fusion.5), channel_id=1, source_target_pairs={{2,4},{3,5},{4,2},{5,3},{10,12},{11,13},{12,10},{13,11},{18,20},{1... | collective-permute-start | bytes 1720328 | tf_op jit(solution)/shard_map/ppermute | solution.py:41
  132.3 58.1 %collective-permute-start.24 = (bf16[80,3584]{1,0:T(8,128)(2,1)S(1)}, bf16[80,3584]{1,0:T(8,128)(2,1)S(1)}, u32[]{:S(2)}, u32[]{:S(2)}) collective-permute-start(bf16[80,3584]{1,0:T(8,128)(2,1)S(1)} %broadcast_select_fusion.1.refs_4_), channel_id=1, source_target_pairs={{0,1},{1,0},{2,3},{3,2},{4,5},{5,4},{6,7},{7,6},{8,9},{9,8},{10,11... | collective-permute-start | bytes 1720328 | tf_op jit(solution)/shard_map/ppermute | solution.py:37
  146.2 26.2 %collective-permute-start.21 = (bf16[80,3584]{1,0:T(8,128)(2,1)S(1)}, bf16[80,3584]{1,0:T(8,128)(2,1)}, u32[]{:S(2)}, u32[]{:S(2)}) collective-permute-start(bf16[80,3584]{1,0:T(8,128)(2,1)S(1)} %add_convert_fusion.4), channel_id=1, source_target_pairs={{2,0},{3,1},{4,6},{5,7},{10,8},{11,9},{12,14},{13,15},{18,16},{19,... | collective-permute-start | bytes 1720328 | tf_op jit(solution)/shard_map/ppermute | solution.py:41
  154.3 15.5 %collective-permute-start.28 = (bf16[320,1024]{1,0:T(8,128)(2,1)S(1)}, bf16[320,1024]{1,0:T(8,128)(2,1)S(1)}, u32[]{:S(2)}, u32[]{:S(2)}) collective-permute-start(bf16[320,1024]{1,0:T(8,128)(2,1)S(1)} %get-tuple-element.20), channel_id=1, source_target_pairs={{0,16},{8,24},{16,0},{24,8},{1,17},{9,25},{17,1},{25,9},{2,18},{10... | collective-permute-start | bytes 1966088 | tf_op jit(solution)/shard_map/ppermute | solution.py:32
  154.6 16.9 %collective-permute-start.26 = (bf16[320,1024]{1,0:T(8,128)(2,1)S(1)}, bf16[320,1024]{1,0:T(8,128)(2,1)S(1)}, u32[]{:S(2)}, u32[]{:S(2)}) collective-permute-start(bf16[320,1024]{1,0:T(8,128)(2,1)S(1)} %get-tuple-element.21), channel_id=1, source_target_pairs={{0,8},{8,0},{16,24},{24,16},{1,9},{9,1},{17,25},{25,17},{2,10},{10... | collective-permute-start | bytes 1966088 | tf_op jit(solution)/shard_map/ppermute | solution.py:32
  169.8 20.6 %collective-permute-start.23 = (bf16[80,3584]{1,0:T(8,128)(2,1)S(1)}, bf16[80,3584]{1,0:T(8,128)(2,1)S(1)}, u32[]{:S(2)}, u32[]{:S(2)}) collective-permute-start(bf16[80,3584]{1,0:T(8,128)(2,1)S(1)} %broadcast_select_fusion.2.refs_3_), channel_id=1, source_target_pairs={{0,1},{1,0},{2,3},{3,2},{4,5},{5,4},{6,7},{7,6},{8,9},{9,8},{10,11... | collective-permute-start | bytes 1720328 | tf_op jit(solution)/shard_map/ppermute | solution.py:37
  172.0 16.2 %collective-permute-start.29 = (bf16[320,1024]{1,0:T(8,128)(2,1)S(1)}, bf16[320,1024]{1,0:T(8,128)(2,1)S(1)}, u32[]{:S(2)}, u32[]{:S(2)}) collective-permute-start(bf16[320,1024]{1,0:T(8,128)(2,1)S(1)} %get-tuple-element.18), channel_id=1, source_target_pairs={{0,8},{8,0},{16,24},{24,16},{1,9},{9,1},{17,25},{25,17},{2,10},{10... | collective-permute-start | bytes 1966088 | tf_op jit(solution)/shard_map/ppermute | solution.py:32
  172.4 17.8 %collective-permute-start.27 = (bf16[320,1024]{1,0:T(8,128)(2,1)S(1)}, bf16[320,1024]{1,0:T(8,128)(2,1)S(1)}, u32[]{:S(2)}, u32[]{:S(2)}) collective-permute-start(bf16[320,1024]{1,0:T(8,128)(2,1)S(1)} %get-tuple-element.19), channel_id=1, source_target_pairs={{0,16},{8,24},{16,0},{24,8},{1,17},{9,25},{17,1},{25,9},{2,18},{10... | collective-permute-start | bytes 1966088 | tf_op jit(solution)/shard_map/ppermute | solution.py:32
  188.2 2.6 %collective-permute-start.25 = (bf16[80,3584]{1,0:T(8,128)(2,1)S(1)}, bf16[80,3584]{1,0:T(8,128)(2,1)S(1)}, u32[]{:S(2)}, u32[]{:S(2)}) collective-permute-start(bf16[80,3584]{1,0:T(8,128)(2,1)S(1)} %broadcast_select_fusion.refs_5_), channel_id=1, source_target_pairs={{0,1},{1,0},{2,3},{3,2},{4,5},{5,4},{6,7},{7,6},{8,9},{9,8},{10,11... | collective-permute-start | bytes 1720328 | tf_op jit(solution)/shard_map/ppermute | solution.py:37
Sparse Core Ops, SparseCore 0:
  13.5 35.8 all-gather.2
where the time goes:
time: 218 us; the launch traced here: 217 us
  waiting for transfers between devices  79.9 us (37%)
  Pallas kernels  67.1 us (31%)
  starting transfers between devices  41.7 us (19%)
  between operations  15 us (7%)
  matrix products  5.85 us (3%)
  other arithmetic  4.89 us (2%)
  local copies, waits for them, and re-layouts  2.3 us (1%)
    pallas_call x4, Pallas kernels, multiply(): pl.pallas_call(multiply_kernel, grid=(width // tile,), in_specs=[pl.Block...  48.1 us
    ppermute x12, waiting for transfers between devices, move_chip(): lax.ppermute(x, 'mp', [(HALVES * a + c, HALVES * b + c) for a, b in pairs...  40.3 us
    ppermute x10, waiting for transfers between devices, swap_quarter(): return lax.ppermute(x, 'dp', [(i, i ^ step) for i in range(size)])  39.1 us
    ppermute x12, starting transfers between devices, move_chip(): lax.ppermute(x, 'mp', [(HALVES * a + c, HALVES * b + c) for a, b in pairs...  22.6 us
    pallas_call x1, Pallas kernels, correct(): pl.pallas_call(lambda *refs: correct_kernel(tokens, *refs), grid=(outs //...  19 us
    ppermute x8, starting transfers between devices, swap_core(): return lax.ppermute(x, 'mp', [(i, i ^ 1) for i in range(size)])  14.2 us
    dot_general x1, matrix products, shards(): act_terms = jnp.dot(act_rows, in_basis, preferred_element_type=jnp.float32)  5.85 us
    ppermute x10, starting transfers between devices, swap_quarter(): return lax.ppermute(x, 'dp', [(i, i ^ step) for i in range(size)])  4.77 us
  transfers between devices with their start and end apart: 31, of which 10 were waited for; matrix products, arithmetic and copies ran while one was open for 5% of the time, Pallas kernels for 22%

commit v1 on v0

v1 whole, which is shorter than its diff:
```python
import jax
import jax.numpy as jnp
from jax import lax
from jax.experimental import pallas as pl
from jax.experimental.pallas import tpu as pltpu
from jax.sharding import PartitionSpec as P

QUARTERS = 4
HALVES = 2
PIECES = QUARTERS * HALVES
MIB = 1 << 20
LANES = 128
DEPTHS = 2


def tile_of(width, limit):
    return max(t for t in range(LANES, limit + 1, LANES) if width % t == 0)


def contract_rows(left, right):
    return lax.dot_general(
        left, right, (((0,), (0,)), ((), ())), preferred_element_type=jnp.float32
    )


def add_rounded(left, right):
    return (left.astype(jnp.float32) + right.astype(jnp.float32)).astype(left.dtype)


class Order:
    def __init__(self):
        self.token = None

    def call(
        self, kernel, operands, out_shape, in_specs=None, out_specs=None, unread=(),
        vmem=6 * MIB, **options,
    ):
        out_shape = list(out_shape)
        whole = pl.BlockSpec(memory_space=pltpu.VMEM)
        anywhere = pl.BlockSpec(memory_space=pl.ANY)
        in_specs = [whole] * len(operands) if in_specs is None else list(in_specs)
        out_specs = [whole] * len(out_shape) if out_specs is None else list(out_specs)
        given, made = len(operands), len(out_shape)
        tokens = [*unread] if self.token is None else [*unread, self.token]

        def body(*refs):
            start = given + len(tokens)
            kernel(*refs[:given], *refs[start:start + made], *refs[start + made + 1:])

        *results, self.token = pl.pallas_call(
            body,
            in_specs=in_specs + [anywhere] * len(tokens),
            out_specs=out_specs + [anywhere],
            out_shape=out_shape + [jax.ShapeDtypeStruct((8, LANES), jnp.float32)],
            compiler_params=pltpu.CompilerParams(vmem_limit_bytes=vmem),
            **options,
        )(*operands, *tokens)
        return results

    def add(self, *pairs, unread=()):
        count = len(pairs)

        def kernel(*refs):
            for i in range(count):
                refs[2 * count + i][...] = add_rounded(refs[2 * i][...], refs[2 * i + 1][...])

        shapes = [jax.ShapeDtypeStruct(x.shape, x.dtype) for x, _ in pairs]
        operands = [x for pair in pairs for x in pair]
        return self.call(kernel, operands, shapes, unread=unread, name="add")

    def pick(self, place, index, first, second):
        def kernel(place_ref, first_ref, second_ref, out_ref):
            @pl.when(place_ref[index] == 0)
            def _():
                out_ref[...] = first_ref[...]

            @pl.when(place_ref[index] != 0)
            def _():
                out_ref[...] = second_ref[...]

        vmem = pl.BlockSpec(memory_space=pltpu.VMEM)
        shape = jax.ShapeDtypeStruct(first.shape, first.dtype)
        in_specs = [pl.BlockSpec(memory_space=pltpu.SMEM), vmem, vmem]
        return self.call(kernel, [place, first, second], [shape], in_specs, name="pick")[0]


def swap_quarter(x, bits):
    size = lax.axis_size("dp")
    step = bits * (size // QUARTERS)
    return lax.ppermute(x, "dp", [(i, i ^ step) for i in range(size)])


def swap_core(x):
    size = lax.axis_size("mp")
    return lax.ppermute(x, "mp", [(i, i ^ 1) for i in range(size)])


def move_chip(x, pairs):
    return lax.ppermute(
        x, "mp", [(HALVES * a + c, HALVES * b + c) for a, b in pairs for c in range(HALVES)]
    )


class LineSum:
    def __init__(self, x):
        chips = lax.axis_size("mp") // HALVES
        last, inner = chips - 1, chips // 2
        self.inward = [[(s, s + 1), (last - s, last - s - 1)] for s in range(inner - 1)]
        self.inward.append([(inner - 1, inner), (inner, inner - 1)])
        self.outward = [
            (s, [(s, s - 1), (last - s, last - s + 1)]) for s in range(inner - 1, 0, -1)
        ]
        self.x, self.hop = x, 0
        self.came = move_chip(x, self.inward[0])

    def add(self, order):
        self.x, = order.add((self.x, self.came))
        self.hop += 1
        inward = self.hop < len(self.inward)
        self.came = move_chip(self.x, self.inward[self.hop] if inward else self.outward[0][1])
        return inward

    def spread(self, order, place):
        for at, (s, _) in enumerate(self.outward):
            self.x = order.pick(place, DEPTHS + s - 1, self.came, self.x)
            if at + 1 < len(self.outward):
                self.came = move_chip(self.x, self.outward[at + 1][1])
        return self.x


def join_rows(order, tokens, queries):
    length, rank = tokens.shape[0] // HALVES, queries.shape[0] // HALVES

    def kernel(tokens_ref, queries_ref, *half_refs):
        for h, ref in enumerate(half_refs):
            ref[:length] = tokens_ref[h * length:(h + 1) * length, :]
            ref[length:] = queries_ref[h * rank:(h + 1) * rank, :]

    shape = jax.ShapeDtypeStruct((length + rank, tokens.shape[1]), tokens.dtype)
    return order.call(kernel, [tokens, queries], [shape] * HALVES, name="join_rows")


def place_rows(place_ref, low_ref, high_ref, rows_ref):
    half = low_ref.shape[0]
    core = place_ref[1]
    rows_ref[pl.ds(pl.multiple_of(core * half, 16), half), :] = low_ref[...]
    rows_ref[pl.ds(pl.multiple_of((1 - core) * half, 16), half), :] = high_ref[...]


def multiply(order, place, low, high, basis, held, unread=()):
    half, depth = low.shape
    width = basis.shape[1]
    tile = tile_of(width, 512)
    first = held is None

    def product(rows_ref, basis_ref, keep_ref, send_ref, columns):
        terms = jnp.dot(
            rows_ref[...], basis_ref[:, columns], preferred_element_type=jnp.float32
        ).astype(keep_ref.dtype)
        keep_ref[:, columns] = terms[:half]
        send_ref[:, columns] = terms[half:]

    def load_kernel(
        place_ref, low_ref, high_ref, basis_ref,
        keep_ref, send_ref, low_out, high_out, held_ref, rows_ref, sems,
    ):
        copies = [
            pltpu.make_async_copy(
                basis_ref.at[:, pl.ds(at, tile)],
                held_ref.at[:, pl.ds(at, tile)],
                sems.at[at // tile],
            )
            for at in range(0, width, tile)
        ]
        for copy in copies:
            copy.start()
        place_rows(place_ref, low_ref, high_ref, rows_ref)
        low_out[...] = low_ref[...]
        high_out[...] = high_ref[...]
        for i, copy in enumerate(copies):
            copy.wait()
            product(rows_ref, held_ref, keep_ref, send_ref, pl.ds(i * tile, tile))

    def held_kernel(place_ref, low_ref, high_ref, held_ref, keep_ref, send_ref, rows_ref):
        place_rows(place_ref, low_ref, high_ref, rows_ref)

        @pl.loop(0, width // tile)
        def _(i):
            columns = pl.ds(pl.multiple_of(i * tile, tile), tile)
            product(rows_ref, held_ref, keep_ref, send_ref, columns)

    smem = pl.BlockSpec(memory_space=pltpu.SMEM)
    vmem = pl.BlockSpec(memory_space=pltpu.VMEM)
    anywhere = pl.BlockSpec(memory_space=pl.ANY)
    out = jax.ShapeDtypeStruct((half, width), low.dtype)
    row = jax.ShapeDtypeStruct((half, depth), low.dtype)
    scratch = [pltpu.VMEM((HALVES * half, depth), low.dtype)]
    if first:
        return order.call(
            load_kernel,
            [place, low, high, basis],
            [out, out, row, row, pltpu.VMEM(basis.shape, basis.dtype)],
            [smem, vmem, vmem, anywhere],
            scratch_shapes=scratch + [pltpu.SemaphoreType.DMA((width // tile,))],
                name="load_and_multiply",
        )
    held = pltpu.with_memory_space_constraint(held, pltpu.VMEM)
    return order.call(
        held_kernel,
        [place, low, high, held],
        [out, out],
        [smem, vmem, vmem, vmem],
        unread=unread,
        scratch_shapes=scratch,
        name="multiply",
    )


def multiply_activations(order, rows, basis, unread=()):
    count, depth = rows.shape
    width, half = basis.shape[1], rows.shape[0] // HALVES
    tile = tile_of(width, 256)

    def kernel(rows_ref, basis_ref, low_ref, high_ref):
        for h, ref in enumerate((low_ref, high_ref)):
            terms = jnp.dot(
                rows_ref[h * half:(h + 1) * half, :],
                basis_ref[...],
                preferred_element_type=jnp.float32,
            )
            ref[...] = terms.astype(ref.dtype)

    out = pl.BlockSpec((half, tile), lambda i: (0, i))
    return order.call(
        kernel,
        [rows, basis],
        [jax.ShapeDtypeStruct((half, width), rows.dtype)] * HALVES,
        [
            pl.BlockSpec((count, depth), lambda i: (0, 0)),
            pl.BlockSpec((depth, tile), lambda i: (0, i)),
        ],
        [out, out],
        unread=unread,
        grid=(width // tile,),
        name="multiply_activations",
    )


def rotated_places(core):
    return [(0, core), (2 - core, core), (1 + core, core), (3, core)]


def correct_kernel(tokens, place_ref, damping_ref, *refs):
    groups = 2 * QUARTERS
    rot_refs, act_refs = refs[:groups], refs[groups:groups + HALVES]
    eig_ref, pre_ref, rot_tok, rot_qry, act_tok, act_qry = refs[groups + HALVES:]
    queries = rot_refs[0].shape[0] - tokens
    quarter, core = place_ref[0], place_ref[1]

    def put(tok, qry, piece, values):
        tok[pl.ds(pl.multiple_of(piece * tokens, 16), tokens), :] = values[:tokens]
        qry[pl.ds(pl.multiple_of(piece * queries, 16), queries), :] = values[tokens:]

    @pl.when(pl.program_id(0) == 0)
    def _():
        per_ref = PIECES // HALVES
        size = tokens + queries
        for piece in range(PIECES):
            at = piece % per_ref * size
            put(act_tok, act_qry, piece, act_refs[piece // per_ref][at:at + size, :])

    for held, refs_held in ((core, rot_refs[:QUARTERS]), (1 - core, rot_refs[QUARTERS:])):
        for (bits, half), ref in zip(rotated_places(held), refs_held):
            put(rot_tok, rot_qry, (quarter ^ bits) * HALVES + half, ref[...])

    length = tokens * PIECES // 2
    total = None
    for seq in range(2):
        rows = slice(seq * length, (seq + 1) * length)
        rotated = contract_rows(rot_tok[rows, :], act_tok[rows, :])
        square = rotated * rotated
        total = square if total is None else total + square
    eig = total * (1.0 / (2 * length))
    eig_ref[...] = eig
    inverse = 1.0 / (eig + damping_ref[0])
    rank = queries * HALVES
    for query in range(QUARTERS):
        rows = slice(query * rank, (query + 1) * rank)
        product = contract_rows(rot_qry[rows, :], act_qry[rows, :])
        pre_ref[query] = (product * inverse).astype(pre_ref.dtype)


def correct(order, tokens, place, damping, rot, act):
    size, outs = rot[0].shape
    rows, ins = act[0].shape
    queries = size - tokens
    tile = tile_of(outs, 256)
    smem = pl.BlockSpec(memory_space=pltpu.SMEM)
    dtype = rot[0].dtype
    return order.call(
        lambda *refs: correct_kernel(tokens, *refs),
        [place, damping, *rot, *act],
        [
            jax.ShapeDtypeStruct((outs, ins), jnp.float32),
            jax.ShapeDtypeStruct((QUARTERS, outs, ins), dtype),
        ],
        [smem, smem]
        + [pl.BlockSpec((size, tile), lambda i: (0, i))] * len(rot)
        + [pl.BlockSpec((rows, ins), lambda i: (0, 0))] * len(act),
        [
            pl.BlockSpec((tile, ins), lambda i: (i, 0)),
            pl.BlockSpec((QUARTERS, tile, ins), lambda i: (0, i, 0)),
        ],
        grid=(outs // tile,),
        scratch_shapes=[
            pltpu.VMEM((PIECES * tokens, tile), dtype),
            pltpu.VMEM((PIECES * queries, tile), dtype),
            pltpu.VMEM((PIECES * tokens, ins), dtype),
            pltpu.VMEM((PIECES * queries, ins), dtype),
        ],
        vmem=32 * MIB,
        name="correct",
    )


def outer_rows(tokens, queries):
    size = lax.axis_size("dp")
    index = lax.axis_index("dp")
    step = 1
    while step < size // QUARTERS:
        pairs = [(i, i ^ step) for i in range(size)]
        first = (index // step) % 2 == 0

        def joined(x):
            other = lax.ppermute(x, "dp", pairs)
            return jnp.where(
                first, jnp.concatenate([x, other]), jnp.concatenate([other, x])
            )

        tokens, queries = joined(tokens), joined(queries)
        step *= 2
    return tokens, queries


class QuarterSum:
    def __init__(self, low, high):
        size = lax.axis_size("dp")
        outer = size // QUARTERS
        self.hops = [(outer, 2 * outer), (2 * outer, outer)]
        step = 1
        while step < outer:
            self.hops.append((step, step))
            step *= 2
        self.size, self.pair, self.hop = size, (low, high), 0
        self.send()

    def send(self):
        self.came = [
            lax.ppermute(x, "dp", [(i, i ^ step) for i in range(self.size)])
            for x, step in zip(self.pair, self.hops[self.hop])
        ]

    def add(self, order):
        self.pair = order.add(*zip(self.pair, self.came))
        self.hop += 1
        if self.hop < len(self.hops):
            self.send()


def activation_rows(inputs, query_in):
    tokens = inputs.shape[0]
    blocks = lax.all_gather(jnp.concatenate([inputs, query_in]), "mp", axis=0)
    holders, _, width = blocks.shape
    if holders != PIECES:
        blocks = jnp.concatenate(
            [
                blocks[:, :tokens].reshape(PIECES, -1, width),
                blocks[:, tokens:].reshape(PIECES, -1, width),
            ],
            axis=1,
        )
    return blocks.reshape(-1, width)


def place_of_device():
    dp, mp = lax.axis_size("dp"), lax.axis_size("mp")
    chips, chip = mp // HALVES, lax.axis_index("mp") // HALVES
    depth = jnp.minimum(chip, chips - 1 - chip)
    values = [lax.axis_index("dp") // (dp // QUARTERS), lax.axis_index("mp") % HALVES]
    values += [jnp.abs(depth - s) for s in range(chips // 2)]
    return jnp.stack(values).astype(jnp.int32)


def shards(out_grads, inputs, out_basis, in_basis, query_out, query_in, damping):
    order = Order()
    place = place_of_device()
    act_rows = activation_rows(inputs, query_in)
    tokens, queries = outer_rows(out_grads, query_out)
    length = tokens.shape[0] // HALVES

    own = join_rows(order, tokens, queries)
    beside = [swap_quarter(own[0], 2), swap_quarter(own[1], 1)]
    own_keep, own_send, *again, held = multiply(order, place, *own, out_basis, None)
    own_came = swap_core(own_send)
    behind = [swap_quarter(again[0], 1), swap_quarter(again[1], 2)]
    across = [swap_quarter(beside[0], 1), swap_quarter(beside[1], 2)]

    def rotate(pair, unread=()):
        keep, send = multiply(order, place, *pair, out_basis, held, unread)
        return keep, swap_core(send)

    def settle(total):
        total = total.spread(order, place)
        return total, swap_core(total)

    def start(keep, came, unread=()):
        return LineSum(order.add((keep, came), unread=unread)[0])

    def inward(line):
        while line.add(order):
            pass

    pair = rotate(beside)
    first = start(own_keep, own_came)
    second = start(*pair)
    pair = rotate(behind)
    first.add(order)
    third = start(*pair, unread=across)
    pair = rotate(across, [second.came])
    acts = QuarterSum(*multiply_activations(order, act_rows, in_basis, [first.came]))
    second.add(order)
    fourth = start(*pair)
    inward(first)
    third.add(order)
    inward(second)
    done = [settle(first)]
    acts.add(order)
    fourth.add(order)
    inward(third)
    done.append(settle(second))
    inward(fourth)
    while acts.hop < len(acts.hops):
        acts.add(order)
    done.append(settle(third))
    done.append(settle(fourth))

    rot = [total for total, _ in done] + [other for _, other in done]
    return tuple(correct(order, length, place, damping, rot, acts.pair))


def solution(mesh):
    placed = (
        P("dp", "mp"),
        P("mp", "dp"),
        P("mp", "dp"),
        P("dp", "mp"),
        P("dp", "mp"),
        P("mp", "dp"),
        P(),
    )
    return jax.shard_map(
        shards,
        mesh=mesh,
        in_specs=placed,
        out_specs=(P("dp", "mp"), P(None, "dp", "mp")),
        check_vma=False,
    )
```

time: 218 us -> 185 us (0.85)
  the two profiles are of different devices: /device:TPU:13 before, /device:TPU:1 now
where the time goes in v1:
time: 185 us; the launch traced here: 184 us
  Pallas kernels  58 us (31%)
  starting transfers between devices  50.8 us (27%)
  waiting for transfers between devices  50.2 us (27%)
  between operations  15.1 us (8%)
  local copies, waits for them, and re-layouts  7.9 us (4%)
    pallas_call x25, Pallas kernels, call(): pl.pallas_call(body, in_specs=in_specs + [anywhere] * len(tokens), out_sp...  58 us
    ppermute x12, waiting for transfers between devices, move_chip(): lax.ppermute(x, 'mp', [(HALVES * a + c, HALVES * b + c) for a, b in pairs...  39.4 us
    ppermute x12, starting transfers between devices, move_chip(): lax.ppermute(x, 'mp', [(HALVES * a + c, HALVES * b + c) for a, b in pairs...  22.6 us
    ppermute x8, starting transfers between devices, swap_core(): return lax.ppermute(x, 'mp', [(i, i ^ 1) for i in range(size)])  18.7 us
    ppermute x6, waiting for transfers between devices, swap_quarter(): return lax.ppermute(x, 'dp', [(i, i ^ step) for i in range(size)])  9.79 us
    unnamed x12, local copies, waits for them, and re-layouts  7.9 us
    ppermute x6, starting transfers between devices, swap_quarter(): return lax.ppermute(x, 'dp', [(i, i ^ step) for i in range(size)])  6.36 us
  transfers between devices with their start and end apart: 31, of which 10 were waited for; matrix products, arithmetic and copies ran while one was open for 0% of the time, Pallas kernels for 21%

profile of v1, /device:TPU:1, one launch (start us, length us, event | category | flops | bytes accessed | tf_op | source)
XLA Modules:
  0.0 183.7 jit_solution(5878805905827079779)
XLA Ops:
  7.2 1.7 pad_maximum_fusion
  9.0 1.2 copy-done.2
  10.2 0.9 copy-done.5
  11.2 2.1 %collective-permute-start.1 = (bf16[80,3584]{1,0:T(8,128)(2,1)S(1)}, bf16[80,3584]{1,0:T(8,128)(2,1)S(1)}, u32[]{:S(2)}, u32[]{:S(2)}) collective-permute-start(bf16[80,3584]{1,0:T(8,128)(2,1)S(1)} %get-tuple-element.63.refs_1_), channel_id=1, source_target_pairs={{0,16},{8,24},{16,0},{24,8},{1,17},{9,25},{17,1},{25,9},{2,18},{10... | collective-permute-start | bytes 1720328 | tf_op jit(solution)/shard_map/ppermute | solution.py:90
  13.3 1.2 collective-permute-start.2
  14.6 10.3 %load_and_multiply.1 = (bf16[80,3584]{1,0:T(8,128)(2,1)S(1)}, bf16[80,3584]{1,0:T(8,128)(2,1)S(1)}, bf16[80,3584]{1,0:T(8,128)(2,1)S(1)}, bf16[80,3584]{1,0:T(8,...) custom-call(s32[4]{0:T(128)S(1)} %pad_add_fusion.refs_0_, ...), custom_call_target="tpu_custom_call" | custom-call | tf_op jit(solution)/shard_map/load_and_multiply/pallas_call | solution.py:50
  24.9 1.3 collective-permute-start
  26.2 0.7 collective-permute-done.2.refs_2_
  26.9 6.0 %multiply.3 = (bf16[80,3584]{1,0:T(8,128)(2,1)S(1)}, bf16[80,3584]{1,0:T(8,128)(2,1)S(1)}, f32[8,128]{1,0:T(8,128)S(1)}) custom-call(s32[4]{0:T(128)S(1)} %pad_add_fusion.refs_0_, bf16[80,3584]{1,0:T(8,128)(2,1)S(1)} %collective-permute-done.1.refs_1_, bf16[80,3584]{1,0:T(8,128)(2,1)S(1)} %collective-permute-done.2.refs_2_, ...), custom_call_target="tpu_custom_call" | custom-call | tf_op jit(solution)/shard_map/multiply/pallas_call | solution.py:50
  32.9 1.8 collective-permute-start.6
  34.8 1.2 collective-permute-start.4
  36.0 0.2 collective-permute-start.5
  36.2 0.1 add.28
  36.4 3.2 %collective-permute-start.3 = (bf16[80,3584]{1,0:T(8,128)(2,1)S(1)}, bf16[80,3584]{1,0:T(8,128)(2,1)S(1)}, u32[]{:S(2)}, u32[]{:S(2)}) collective-permute-start(bf16[80,3584]{1,0:T(8,128)(2,1)S(1)} %get-tuple-element.71.refs_0_), channel_id=1, source_target_pairs={{0,2},{1,3},{6,4},{7,5},{8,10},{9,11},{14,12},{15,13},{16,18},{17,... | collective-permute-start | bytes 1720328 | tf_op jit(solution)/shard_map/ppermute | solution.py:99
  39.6 0.3 collective-permute-start.8
  39.9 1.2 collective-permute-start.9
  41.3 8.0 %collective-permute-done.4.refs_1_ = bf16[80,3584]{1,0:T(8,128)(2,1)S(1)} collective-permute-done((bf16[80,3584]{1,0:T(8,128)(2,1)S(1)}, bf16[80,3584]{1,0:T(8,128)(2,1)S(1)}, u32[]{:S(2)}, u32[]{:S(2)}) %collective-permute-start.4) | collective-permute-done | bytes 573472 | tf_op jit(solution)/shard_map/ppermute | solution.py:90
  49.3 0.9 collective-permute-done.5.refs_2_
  50.2 6.0 %multiply.4 = (bf16[80,3584]{1,0:T(8,128)(2,1)S(1)}, bf16[80,3584]{1,0:T(8,128)(2,1)S(1)}, f32[8,128]{1,0:T(8,128)S(1)}) custom-call(s32[4]{0:T(128)S(1)} %pad_add_fusion.refs_0_, bf16[80,3584]{1,0:T(8,128)(2,1)S(1)} %collective-permute-done.4.refs_1_, bf16[80,3584]{1,0:T(8,128)(2,1)S(1)} %collective-permute-done.5.refs_2_, ...), custom_call_target="tpu_custom_call" | custom-call | tf_op jit(solution)/shard_map/multiply/pallas_call | solution.py:50
  56.2 2.0 %collective-permute-start.11 = (bf16[80,3584]{1,0:T(8,128)(2,1)S(1)}, bf16[80,3584]{1,0:T(8,128)(2,1)S(1)}, u32[]{:S(2)}, u32[]{:S(2)}) collective-permute-start(bf16[80,3584]{1,0:T(8,128)(2,1)S(1)} %get-tuple-element.82), channel_id=1, source_target_pairs={{0,1},{1,0},{2,3},{3,2},{4,5},{5,4},{6,7},{7,6},{8,9},{9,8},{10,11... | collective-permute-start | bytes 1720328 | tf_op jit(solution)/shard_map/ppermute | solution.py:95
  58.2 3.2 %collective-permute-start.10 = (bf16[80,3584]{1,0:T(8,128)(2,1)S(1)}, bf16[80,3584]{1,0:T(8,128)(2,1)S(1)}, u32[]{:S(2)}, u32[]{:S(2)}) collective-permute-start(bf16[80,3584]{1,0:T(8,128)(2,1)S(1)} %get-tuple-element.80.refs_0_), channel_id=1, source_target_pairs={{0,2},{1,3},{6,4},{7,5},{8,10},{9,11},{14,12},{15,13},{16,18},{17,... | collective-permute-start | bytes 1720328 | tf_op jit(solution)/shard_map/ppermute | solution.py:99
  61.4 0.1 add.30
  61.6 0.7 collective-permute-start.7
  62.3 0.2 collective-permute-done.9.refs_3_.refs_2_
  62.6 11.1 %collective-permute-done.10.refs_4_.refs_1_ = bf16[80,3584]{1,0:T(8,128)(2,1)S(1)} collective-permute-done((bf16[80,3584]{1,0:T(8,128)(2,1)S(1)}, bf16[80,3584]{1,0:T(8,128)(2,1)S(1)}, u32[]{:S(2)}, u32[]{:S(2)}) %collective-permute-start.10) | collective-permute-done | bytes 573472 | tf_op jit(solution)/shard_map/ppermute | solution.py:99
  73.8 6.8 %multiply.5 = (bf16[80,3584]{1,0:T(8,128)(2,1)S(1)}, bf16[80,3584]{1,0:T(8,128)(2,1)}, f32[8,128]{1,0:T(8,128)S(1)}) custom-call(s32[4]{0:T(128)S(1)} %pad_add_fusion.refs_0_, bf16[80,3584]{1,0:T(8,128)(2,1)S(1)} %collective-permute-done.8.refs_2_.refs_1_, bf16[80,3584]{1,0:T(8,128)(2,1)S(1)} %collective-permute-done.9.refs_3_.refs_2_, ...), custom_call_target="tpu_custom_call" | custom-call | tf_op jit(solution)/shard_map/multiply/pallas_call | solution.py:50
  80.6 0.8 copy-done.3
  81.4 0.8 collective-permute-start.12
  82.2 4.1 %collective-permute-start.15 = (bf16[80,3584]{1,0:T(8,128)(2,1)S(1)}, bf16[80,3584]{1,0:T(8,128)(2,1)S(1)}, u32[]{:S(2)}, u32[]{:S(2)}) collective-permute-start(bf16[80,3584]{1,0:T(8,128)(2,1)S(1)} %get-tuple-element.93.refs_0_), channel_id=1, source_target_pairs={{0,2},{1,3},{6,4},{7,5},{8,10},{9,11},{14,12},{15,13},{16,18},{17,... | collective-permute-start | bytes 1720328 | tf_op jit(solution)/shard_map/ppermute | solution.py:99
  86.4 2.2 %copy-done = bf16[2048,1024]{1,0:T(8,128)(2,1)S(1)} copy-done((bf16[2048,1024]{1,0:T(8,128)(2,1)S(1)}, bf16[2048,1024]{1,0:T(8,128)(2,1)}, u32[]{:S(2)}) %copy-start) | copy-done | bytes 4194328
  88.6 1.7 copy-done.1
  90.3 4.1 %multiply_activations.1 = (bf16[320,1024]{1,0:T(8,128)(2,1)S(1)}, bf16[320,1024]{1,0:T(8,128)(2,1)S(1)}, f32[8,128]{1,0:T(8,128)S(1)}) custom-call(bf16[640,2048]{1,0:T(8,128)(2,1)S(1)} %copy-done.1, bf16[2048,1024]{1,0:T(8,128)(2,1)S(1)} %copy-done, bf16[80,3584]{1,0:T(8,128)(2,1)S(1)} %collective-permute-done.7.refs_2_.refs_1_, ...), custom_call_target="tpu_custom_call" | custom-call | tf_op jit(solution)/shard_map/multiply_activations/pallas_call | solution.py:50
  94.4 0.3 collective-permute-start.19
  94.7 0.2 collective-permute-start.20
  95.1 0.7 collective-permute-start.14
  95.8 1.1 copy-done.4
  96.9 1.2 add.33
  98.1 0.1 add.34
  98.2 1.3 collective-permute-start.13
  99.5 4.1 %collective-permute-start.18 = (bf16[80,3584]{1,0:T(8,128)(2,1)S(1)}, bf16[80,3584]{1,0:T(8,128)(2,1)S(1)}, u32[]{:S(2)}, u32[]{:S(2)}) collective-permute-start(bf16[80,3584]{1,0:T(8,128)(2,1)S(1)} %get-tuple-element.100.refs_0_), channel_id=1, source_target_pairs={{0,2},{1,3},{6,4},{7,5},{8,10},{9,11},{14,12},{15,13},{16,18},{17,... | collective-permute-start | bytes 1720328 | tf_op jit(solution)/shard_map/ppermute | solution.py:99
  103.6 0.1 add.35
  103.7 0.7 collective-permute-start.17
  104.6 9.2 %collective-permute-done.13.refs_1_ = bf16[80,3584]{1,0:T(8,128)(2,1)S(1)} collective-permute-done((bf16[80,3584]{1,0:T(8,128)(2,1)S(1)}, bf16[80,3584]{1,0:T(8,128)(2,1)S(1)}, u32[]{:S(2)}, u32[]{:S(2)}) %collective-permute-start.13) | collective-permute-done | bytes 573472 | tf_op jit(solution)/shard_map/ppermute | solution.py:99
  113.7 1.3 collective-permute-start.16
  115.0 0.6 pick.4
  115.7 0.3 add.37
  116.0 0.2 add.38
  116.2 0.7 collective-permute-start.24
  116.9 1.3 collective-permute-start.22
  118.2 1.2 collective-permute-start.23
  119.5 1.3 collective-permute-start.21
  120.8 7.5 %collective-permute-done.16.refs_1_ = bf16[80,3584]{1,0:T(8,128)(2,1)S(1)} collective-permute-done((bf16[80,3584]{1,0:T(8,128)(2,1)S(1)}, bf16[80,3584]{1,0:T(8,128)(2,1)S(1)}, u32[]{:S(2)}, u32[]{:S(2)}) %collective-permute-start.16) | collective-permute-done | bytes 573472 | tf_op jit(solution)/shard_map/ppermute | solution.py:99
  128.4 0.6 pick.5
  129.1 1.3 collective-permute-start.25
  130.4 5.0 %collective-permute-start.26 = (bf16[80,3584]{1,0:T(8,128)(2,1)S(1)}, bf16[80,3584]{1,0:T(8,128)(2,1)S(1)}, u32[]{:S(2)}, u32[]{:S(2)}) collective-permute-start(bf16[80,3584]{1,0:T(8,128)(2,1)S(1)} %get-tuple-element.97.refs_2_), channel_id=1, source_target_pairs={{0,1},{1,0},{2,3},{3,2},{4,5},{5,4},{6,7},{7,6},{8,9},{9,8},{10,11... | collective-permute-start | bytes 1720328 | tf_op jit(solution)/shard_map/ppermute | solution.py:95
  135.5 0.3 add.41
  135.8 4.9 %collective-permute-done.21.refs_1_ = bf16[80,3584]{1,0:T(8,128)(2,1)S(1)} collective-permute-done((bf16[80,3584]{1,0:T(8,128)(2,1)S(1)}, bf16[80,3584]{1,0:T(8,128)(2,1)S(1)}, u32[]{:S(2)}, u32[]{:S(2)}) %collective-permute-start.21) | collective-permute-done | bytes 573472 | tf_op jit(solution)/shard_map/ppermute | solution.py:99
  140.7 0.6 pick.6
  141.2 5.0 %collective-permute-start.28 = (bf16[80,3584]{1,0:T(8,128)(2,1)S(1)}, bf16[80,3584]{1,0:T(8,128)(2,1)S(1)}, u32[]{:S(2)}, u32[]{:S(2)}) collective-permute-start(bf16[80,3584]{1,0:T(8,128)(2,1)S(1)} %get-tuple-element.115.refs_4_), channel_id=1, source_target_pairs={{0,1},{1,0},{2,3},{3,2},{4,5},{5,4},{6,7},{7,6},{8,9},{9,8},{10,11... | collective-permute-start | bytes 1720328 | tf_op jit(solution)/shard_map/ppermute | solution.py:95
  146.2 6.7 %collective-permute-done.25.refs_1_ = bf16[80,3584]{1,0:T(8,128)(2,1)S(1)} collective-permute-done((bf16[80,3584]{1,0:T(8,128)(2,1)S(1)}, bf16[80,3584]{1,0:T(8,128)(2,1)S(1)}, u32[]{:S(2)}, u32[]{:S(2)}) %collective-permute-start.25) | collective-permute-done | bytes 573472 | tf_op jit(solution)/shard_map/ppermute | solution.py:99
  152.9 0.6 pick.7
  153.5 2.7 %collective-permute-start.29 = (bf16[80,3584]{1,0:T(8,128)(2,1)S(1)}, bf16[80,3584]{1,0:T(8,128)(2,1)S(1)}, u32[]{:S(2)}, u32[]{:S(2)}) collective-permute-start(bf16[80,3584]{1,0:T(8,128)(2,1)S(1)} %get-tuple-element.118.refs_5_), channel_id=1, source_target_pairs={{0,1},{1,0},{2,3},{3,2},{4,5},{5,4},{6,7},{7,6},{8,9},{9,8},{10,11... | collective-permute-start | bytes 1720328 | tf_op jit(solution)/shard_map/ppermute | solution.py:95
  156.9 0.9 collective-permute-done.29.refs_9_
  157.9 19.0 %correct.1 = (f32[3584,1024]{1,0:T(8,128)}, bf16[4,3584,1024]{2,1,0:T(8,128)(2,1)}, f32[8,128]{1,0:T(8,128)}) custom-call(s32[4]{0:T(128)S(1)} %pad_add_fusion.refs_0_, f32[1]{0:T(128)S(6)} %copy.9.refs_1_, bf16[80,3584]{1,0:T(8,128)(2,1)S(1)} %get-tuple-element.97.refs_2_, bf16[80,3584]{1,0:T(8,128)(2,1)S(1)} %get-tuple-element.107.refs_3_, ...), custom_call_target="tpu_custom_call" | custom-call | tf_op jit(solution)/shard_map/correct/pallas_call | solution.py:50
  (38 shorter events, 1.2 us)
Async XLA Ops:
  7.2 79.2 %all-gather.3.cloned.1.call-start = ((), (), s32[]{:S(2)}) async-start(), calls=%async_computation | async-start | bytes 2949120 | tf_op jit(solution)/shard_map/all_gather | solution.py:372
  9.0 1.2 copy-start.2
  10.2 0.9 copy-start.5
  11.2 15.1 %collective-permute-start.1 = (bf16[80,3584]{1,0:T(8,128)(2,1)S(1)}, bf16[80,3584]{1,0:T(8,128)(2,1)S(1)}, u32[]{:S(2)}, u32[]{:S(2)}) collective-permute-start(bf16[80,3584]{1,0:T(8,128)(2,1)S(1)} %get-tuple-element.63.refs_1_), channel_id=1, source_target_pairs={{0,16},{8,24},{16,0},{24,8},{1,17},{9,25},{17,1},{25,9},{2,18},{10... | collective-permute-start | bytes 1720328 | tf_op jit(solution)/shard_map/ppermute | solution.py:90
  13.3 13.6 %collective-permute-start.2 = (bf16[80,3584]{1,0:T(8,128)(2,1)S(1)}, bf16[80,3584]{1,0:T(8,128)(2,1)S(1)}, u32[]{:S(2)}, u32[]{:S(2)}) collective-permute-start(bf16[80,3584]{1,0:T(8,128)(2,1)S(1)} %get-tuple-element.64.refs_2_), channel_id=1, source_target_pairs={{0,8},{8,0},{16,24},{24,16},{1,9},{9,1},{17,25},{25,17},{2,10},{10... | collective-permute-start | bytes 1720328 | tf_op jit(solution)/shard_map/ppermute | solution.py:90
  24.9 11.3 %collective-permute-start = (bf16[80,3584]{1,0:T(8,128)(2,1)S(1)}, bf16[80,3584]{1,0:T(8,128)(2,1)S(1)}, u32[]{:S(2)}, u32[]{:S(2)}) collective-permute-start(bf16[80,3584]{1,0:T(8,128)(2,1)S(1)} %get-tuple-element.67), channel_id=1, source_target_pairs={{0,1},{1,0},{2,3},{3,2},{4,5},{5,4},{6,7},{7,6},{8,9},{9,8},{10,11... | collective-permute-start | bytes 1720328 | tf_op jit(solution)/shard_map/ppermute | solution.py:95
  32.9 7.0 %collective-permute-start.6 = (bf16[80,3584]{1,0:T(8,128)(2,1)S(1)}, bf16[80,3584]{1,0:T(8,128)(2,1)S(1)}, u32[]{:S(2)}, u32[]{:S(2)}) collective-permute-start(bf16[80,3584]{1,0:T(8,128)(2,1)S(1)} %get-tuple-element.75), channel_id=1, source_target_pairs={{0,1},{1,0},{2,3},{3,2},{4,5},{5,4},{6,7},{7,6},{8,9},{9,8},{10,11... | collective-permute-start | bytes 1720328 | tf_op jit(solution)/shard_map/ppermute | solution.py:95
  34.8 14.6 %collective-permute-start.4 = (bf16[80,3584]{1,0:T(8,128)(2,1)S(1)}, bf16[80,3584]{1,0:T(8,128)(2,1)S(1)}, u32[]{:S(2)}, u32[]{:S(2)}) collective-permute-start(bf16[80,3584]{1,0:T(8,128)(2,1)S(1)} %get-tuple-element.72), channel_id=1, source_target_pairs={{0,8},{8,0},{16,24},{24,16},{1,9},{9,1},{17,25},{25,17},{2,10},{10... | collective-permute-start | bytes 1720328 | tf_op jit(solution)/shard_map/ppermute | solution.py:90
  36.0 14.2 %collective-permute-start.5 = (bf16[80,3584]{1,0:T(8,128)(2,1)S(1)}, bf16[80,3584]{1,0:T(8,128)(2,1)S(1)}, u32[]{:S(2)}, u32[]{:S(2)}) collective-permute-start(bf16[80,3584]{1,0:T(8,128)(2,1)S(1)} %get-tuple-element.73), channel_id=1, source_target_pairs={{0,16},{8,24},{16,0},{24,8},{1,17},{9,25},{17,1},{25,9},{2,18},{10... | collective-permute-start | bytes 1720328 | tf_op jit(solution)/shard_map/ppermute | solution.py:90
  36.4 25.1 %collective-permute-start.3 = (bf16[80,3584]{1,0:T(8,128)(2,1)S(1)}, bf16[80,3584]{1,0:T(8,128)(2,1)S(1)}, u32[]{:S(2)}, u32[]{:S(2)}) collective-permute-start(bf16[80,3584]{1,0:T(8,128)(2,1)S(1)} %get-tuple-element.71.refs_0_), channel_id=1, source_target_pairs={{0,2},{1,3},{6,4},{7,5},{8,10},{9,11},{14,12},{15,13},{16,18},{17,... | collective-permute-start | bytes 1720328 | tf_op jit(solution)/shard_map/ppermute | solution.py:99
  39.6 22.7 %collective-permute-start.8 = (bf16[80,3584]{1,0:T(8,128)(2,1)S(1)}, bf16[80,3584]{1,0:T(8,128)(2,1)S(1)}, u32[]{:S(2)}, u32[]{:S(2)}) collective-permute-start(bf16[80,3584]{1,0:T(8,128)(2,1)S(1)} %collective-permute-done.1.refs_1_), channel_id=1, source_target_pairs={{0,8},{8,0},{16,24},{24,16},{1,9},{9,1},{17,25},{25,17},{2,10},{10... | collective-permute-start | bytes 1720328 | tf_op jit(solution)/shard_map/ppermute | solution.py:90
  39.9 22.6 %collective-permute-start.9 = (bf16[80,3584]{1,0:T(8,128)(2,1)S(1)}, bf16[80,3584]{1,0:T(8,128)(2,1)S(1)}, u32[]{:S(2)}, u32[]{:S(2)}) collective-permute-start(bf16[80,3584]{1,0:T(8,128)(2,1)S(1)} %collective-permute-done.2.refs_2_), channel_id=1, source_target_pairs={{0,16},{8,24},{16,0},{24,8},{1,17},{9,25},{17,1},{25,9},{2,18},{10... | collective-permute-start | bytes 1720328 | tf_op jit(solution)/shard_map/ppermute | solution.py:90
  56.2 6.3 %collective-permute-start.11 = (bf16[80,3584]{1,0:T(8,128)(2,1)S(1)}, bf16[80,3584]{1,0:T(8,128)(2,1)S(1)}, u32[]{:S(2)}, u32[]{:S(2)}) collective-permute-start(bf16[80,3584]{1,0:T(8,128)(2,1)S(1)} %get-tuple-element.82), channel_id=1, source_target_pairs={{0,1},{1,0},{2,3},{3,2},{4,5},{5,4},{6,7},{7,6},{8,9},{9,8},{10,11... | collective-permute-start | bytes 1720328 | tf_op jit(solution)/shard_map/ppermute | solution.py:95
  58.2 15.6 %collective-permute-start.10 = (bf16[80,3584]{1,0:T(8,128)(2,1)S(1)}, bf16[80,3584]{1,0:T(8,128)(2,1)S(1)}, u32[]{:S(2)}, u32[]{:S(2)}) collective-permute-start(bf16[80,3584]{1,0:T(8,128)(2,1)S(1)} %get-tuple-element.80.refs_0_), channel_id=1, source_target_pairs={{0,2},{1,3},{6,4},{7,5},{8,10},{9,11},{14,12},{15,13},{16,18},{17,... | collective-permute-start | bytes 1720328 | tf_op jit(solution)/shard_map/ppermute | solution.py:99
  61.6 24.7 %collective-permute-start.7 = (bf16[80,3584]{1,0:T(8,128)(2,1)S(1)}, bf16[80,3584]{1,0:T(8,128)(2,1)S(1)}, u32[]{:S(2)}, u32[]{:S(2)}) collective-permute-start(bf16[80,3584]{1,0:T(8,128)(2,1)S(1)} %get-tuple-element.79.refs_0_), channel_id=1, source_target_pairs={{2,4},{3,5},{4,2},{5,3},{10,12},{11,13},{12,10},{13,11},{18,20},{1... | collective-permute-start | bytes 1720328 | tf_op jit(solution)/shard_map/ppermute | solution.py:99
  80.6 0.8 copy-start.3
  81.4 14.4 %collective-permute-start.12 = (bf16[80,3584]{1,0:T(8,128)(2,1)}, bf16[80,3584]{1,0:T(8,128)(2,1)}, u32[]{:S(2)}, u32[]{:S(2)}) collective-permute-start(bf16[80,3584]{1,0:T(8,128)(2,1)} %get-tuple-element.86), channel_id=1, source_target_pairs={{0,1},{1,0},{2,3},{3,2},{4,5},{5,4},{6,7},{7,6},{8,9},{9,8},{10,11... | collective-permute-start | bytes 1720328 | tf_op jit(solution)/shard_map/ppermute | solution.py:95
  82.2 17.3 %collective-permute-start.15 = (bf16[80,3584]{1,0:T(8,128)(2,1)S(1)}, bf16[80,3584]{1,0:T(8,128)(2,1)S(1)}, u32[]{:S(2)}, u32[]{:S(2)}) collective-permute-start(bf16[80,3584]{1,0:T(8,128)(2,1)S(1)} %get-tuple-element.93.refs_0_), channel_id=1, source_target_pairs={{0,2},{1,3},{6,4},{7,5},{8,10},{9,11},{14,12},{15,13},{16,18},{17,... | collective-permute-start | bytes 1720328 | tf_op jit(solution)/shard_map/ppermute | solution.py:99
  86.4 2.2 %copy-start = (bf16[2048,1024]{1,0:T(8,128)(2,1)S(1)}, bf16[2048,1024]{1,0:T(8,128)(2,1)}, u32[]{:S(2)}) copy-start(bf16[2048,1024]{1,0:T(8,128)(2,1)} %refs_1_.4) | copy-start | bytes 12582916
  88.6 1.7 copy-start.1
  94.4 21.2 %collective-permute-start.19 = (bf16[320,1024]{1,0:T(8,128)(2,1)S(1)}, bf16[320,1024]{1,0:T(8,128)(2,1)S(1)}, u32[]{:S(2)}, u32[]{:S(2)}) collective-permute-start(bf16[320,1024]{1,0:T(8,128)(2,1)S(1)} %get-tuple-element.101.refs_0_), channel_id=1, source_target_pairs={{0,8},{8,0},{16,24},{24,16},{1,9},{9,1},{17,25},{25,17},{2,10},{10... | collective-permute-start | bytes 1966088 | tf_op jit(solution)/shard_map/ppermute | solution.py:359
  94.7 20.9 %collective-permute-start.20 = (bf16[320,1024]{1,0:T(8,128)(2,1)S(1)}, bf16[320,1024]{1,0:T(8,128)(2,1)S(1)}, u32[]{:S(2)}, u32[]{:S(2)}) collective-permute-start(bf16[320,1024]{1,0:T(8,128)(2,1)S(1)} %get-tuple-element.102.refs_2_), channel_id=1, source_target_pairs={{0,16},{8,24},{16,0},{24,8},{1,17},{9,25},{17,1},{25,9},{2,18},{10... | collective-permute-start | bytes 1966088 | tf_op jit(solution)/shard_map/ppermute | solution.py:359
  95.1 8.6 %collective-permute-start.14 = (bf16[80,3584]{1,0:T(8,128)(2,1)S(1)}, bf16[80,3584]{1,0:T(8,128)(2,1)S(1)}, u32[]{:S(2)}, u32[]{:S(2)}) collective-permute-start(bf16[80,3584]{1,0:T(8,128)(2,1)S(1)} %get-tuple-element.92.refs_0_), channel_id=1, source_target_pairs={{2,4},{3,5},{4,2},{5,3},{10,12},{11,13},{12,10},{13,11},{18,20},{1... | collective-permute-start | bytes 1720328 | tf_op jit(solution)/shard_map/ppermute | solution.py:99
  95.8 1.1 copy-start.4
  98.2 15.5 %collective-permute-start.13 = (bf16[80,3584]{1,0:T(8,128)(2,1)S(1)}, bf16[80,3584]{1,0:T(8,128)(2,1)S(1)}, u32[]{:S(2)}, u32[]{:S(2)}) collective-permute-start(bf16[80,3584]{1,0:T(8,128)(2,1)S(1)} %get-tuple-element.91.refs_2_), channel_id=1, source_target_pairs={{2,0},{3,1},{4,6},{5,7},{10,8},{11,9},{12,14},{13,15},{18,16},{19,... | collective-permute-start | bytes 1720328 | tf_op jit(solution)/shard_map/ppermute | solution.py:99
  99.5 16.5 %collective-permute-start.18 = (bf16[80,3584]{1,0:T(8,128)(2,1)S(1)}, bf16[80,3584]{1,0:T(8,128)(2,1)S(1)}, u32[]{:S(2)}, u32[]{:S(2)}) collective-permute-start(bf16[80,3584]{1,0:T(8,128)(2,1)S(1)} %get-tuple-element.100.refs_0_), channel_id=1, source_target_pairs={{0,2},{1,3},{6,4},{7,5},{8,10},{9,11},{14,12},{15,13},{16,18},{17,... | collective-permute-start | bytes 1720328 | tf_op jit(solution)/shard_map/ppermute | solution.py:99
  103.7 15.7 %collective-permute-start.17 = (bf16[80,3584]{1,0:T(8,128)(2,1)S(1)}, bf16[80,3584]{1,0:T(8,128)(2,1)S(1)}, u32[]{:S(2)}, u32[]{:S(2)}) collective-permute-start(bf16[80,3584]{1,0:T(8,128)(2,1)S(1)} %get-tuple-element.99.refs_0_), channel_id=1, source_target_pairs={{2,4},{3,5},{4,2},{5,3},{10,12},{11,13},{12,10},{13,11},{18,20},{1... | collective-permute-start | bytes 1720328 | tf_op jit(solution)/shard_map/ppermute | solution.py:99
  113.7 14.6 %collective-permute-start.16 = (bf16[80,3584]{1,0:T(8,128)(2,1)S(1)}, bf16[80,3584]{1,0:T(8,128)(2,1)S(1)}, u32[]{:S(2)}, u32[]{:S(2)}) collective-permute-start(bf16[80,3584]{1,0:T(8,128)(2,1)S(1)} %get-tuple-element.98.refs_2_), channel_id=1, source_target_pairs={{2,0},{3,1},{4,6},{5,7},{10,8},{11,9},{12,14},{13,15},{18,16},{19,... | collective-permute-start | bytes 1720328 | tf_op jit(solution)/shard_map/ppermute | solution.py:99
  116.2 12.8 %collective-permute-start.24 = (bf16[80,3584]{1,0:T(8,128)(2,1)S(1)}, bf16[80,3584]{1,0:T(8,128)(2,1)S(1)}, u32[]{:S(2)}, u32[]{:S(2)}) collective-permute-start(bf16[80,3584]{1,0:T(8,128)(2,1)S(1)} %get-tuple-element.111.refs_0_), channel_id=1, source_target_pairs={{2,4},{3,5},{4,2},{5,3},{10,12},{11,13},{12,10},{13,11},{18,20},{1... | collective-permute-start | bytes 1720328 | tf_op jit(solution)/shard_map/ppermute | solution.py:99
  116.9 18.5 %collective-permute-start.22 = (bf16[320,1024]{1,0:T(8,128)(2,1)S(1)}, bf16[320,1024]{1,0:T(8,128)(2,1)S(1)}, u32[]{:S(2)}, u32[]{:S(2)}) collective-permute-start(bf16[320,1024]{1,0:T(8,128)(2,1)S(1)} %get-tuple-element.109.refs_0_), channel_id=1, source_target_pairs={{0,16},{8,24},{16,0},{24,8},{1,17},{9,25},{17,1},{25,9},{2,18},{10... | collective-permute-start | bytes 1966088 | tf_op jit(solution)/shard_map/ppermute | solution.py:359
  118.2 17.3 %collective-permute-start.23 = (bf16[320,1024]{1,0:T(8,128)(2,1)S(1)}, bf16[320,1024]{1,0:T(8,128)(2,1)S(1)}, u32[]{:S(2)}, u32[]{:S(2)}) collective-permute-start(bf16[320,1024]{1,0:T(8,128)(2,1)S(1)} %get-tuple-element.110.refs_2_), channel_id=1, source_target_pairs={{0,8},{8,0},{16,24},{24,16},{1,9},{9,1},{17,25},{25,17},{2,10},{10... | collective-permute-start | bytes 1966088 | tf_op jit(solution)/shard_map/ppermute | solution.py:359
  119.5 21.1 %collective-permute-start.21 = (bf16[80,3584]{1,0:T(8,128)(2,1)S(1)}, bf16[80,3584]{1,0:T(8,128)(2,1)S(1)}, u32[]{:S(2)}, u32[]{:S(2)}) collective-permute-start(bf16[80,3584]{1,0:T(8,128)(2,1)S(1)} %get-tuple-element.108.refs_2_), channel_id=1, source_target_pairs={{2,0},{3,1},{4,6},{5,7},{10,8},{11,9},{12,14},{13,15},{18,16},{19,... | collective-permute-start | bytes 1720328 | tf_op jit(solution)/shard_map/ppermute | solution.py:99
  129.1 23.8 %collective-permute-start.25 = (bf16[80,3584]{1,0:T(8,128)(2,1)S(1)}, bf16[80,3584]{1,0:T(8,128)(2,1)S(1)}, u32[]{:S(2)}, u32[]{:S(2)}) collective-permute-start(bf16[80,3584]{1,0:T(8,128)(2,1)S(1)} %get-tuple-element.116.refs_2_), channel_id=1, source_target_pairs={{2,0},{3,1},{4,6},{5,7},{10,8},{11,9},{12,14},{13,15},{18,16},{19,... | collective-permute-start | bytes 1720328 | tf_op jit(solution)/shard_map/ppermute | solution.py:99
  130.4 26.5 %collective-permute-start.26 = (bf16[80,3584]{1,0:T(8,128)(2,1)S(1)}, bf16[80,3584]{1,0:T(8,128)(2,1)S(1)}, u32[]{:S(2)}, u32[]{:S(2)}) collective-permute-start(bf16[80,3584]{1,0:T(8,128)(2,1)S(1)} %get-tuple-element.97.refs_2_), channel_id=1, source_target_pairs={{0,1},{1,0},{2,3},{3,2},{4,5},{5,4},{6,7},{7,6},{8,9},{9,8},{10,11... | collective-permute-start | bytes 1720328 | tf_op jit(solution)/shard_map/ppermute | solution.py:95
  135.4 21.5 %collective-permute-start.27 = (bf16[80,3584]{1,0:T(8,128)(2,1)S(1)}, bf16[80,3584]{1,0:T(8,128)(2,1)S(1)}, u32[]{:S(2)}, u32[]{:S(2)}) collective-permute-start(bf16[80,3584]{1,0:T(8,128)(2,1)S(1)} %get-tuple-element.107.refs_3_), channel_id=1, source_target_pairs={{0,1},{1,0},{2,3},{3,2},{4,5},{5,4},{6,7},{7,6},{8,9},{9,8},{10,11... | collective-permute-start | bytes 1720328 | tf_op jit(solution)/shard_map/ppermute | solution.py:95
  141.2 15.7 %collective-permute-start.28 = (bf16[80,3584]{1,0:T(8,128)(2,1)S(1)}, bf16[80,3584]{1,0:T(8,128)(2,1)S(1)}, u32[]{:S(2)}, u32[]{:S(2)}) collective-permute-start(bf16[80,3584]{1,0:T(8,128)(2,1)S(1)} %get-tuple-element.115.refs_4_), channel_id=1, source_target_pairs={{0,1},{1,0},{2,3},{3,2},{4,5},{5,4},{6,7},{7,6},{8,9},{9,8},{10,11... | collective-permute-start | bytes 1720328 | tf_op jit(solution)/shard_map/ppermute | solution.py:95
  153.5 4.3 %collective-permute-start.29 = (bf16[80,3584]{1,0:T(8,128)(2,1)S(1)}, bf16[80,3584]{1,0:T(8,128)(2,1)S(1)}, u32[]{:S(2)}, u32[]{:S(2)}) collective-permute-start(bf16[80,3584]{1,0:T(8,128)(2,1)S(1)} %get-tuple-element.118.refs_5_), channel_id=1, source_target_pairs={{0,1},{1,0},{2,3},{3,2},{4,5},{5,4},{6,7},{7,6},{8,9},{9,8},{10,11... | collective-permute-start | bytes 1720328 | tf_op jit(solution)/shard_map/ppermute | solution.py:95
Sparse Core Ops, SparseCore 0:
  9.6 35.6 all-gather.2
